TPU v7x, 256 devices: a whole 4x4x8 slice. The times are simulated.
256 devices in a mesh: tile: 64 (over x, z, core), mode: 4 (over y).
Axes of the slice: x: 4, y: 4, z: 8, core: 2. Of those that a mesh axis runs over, the one named last changes fastest.
Arguments:
- object_tile: float32 [2, 384, 16384], P(None, None, 'tile'), may hold values from -6 to 6
- probe: float32 [12, 2, 256, 256], P('mode'), may hold values from -0.9 to 0.9
- amplitudes: float32 [128, 256, 256], P('tile'), may hold values from 0 to 2
- row_offsets: int32 [128], P('tile'), may hold values from 0 to 128
- col_offsets: int32 [128], P('tile'), may hold values from 0 to 255
- scan_count: int32 [64], P('tile'), may hold values from 1 to 2
Outputs:
- object_new: float32 [2, 384, 16384], P(None, None, 'tile')
- probe_new: float32 [12, 2, 256, 256], P('mode')
All inputs are finite; a program needn't handle non-finite values.
Results may differ from a plain program's by a relative error of at most 0.011.
Values sent between devices are 32-bit elements; how exact they have to be, the bound alone decides.
A program may use at most 64 MiB of HBM per device.

v0:
```python
import jax
import jax.numpy as jnp
from jax import lax
from jax.sharding import PartitionSpec as P


def passed_along(value, axis, steps):
    count = lax.axis_size(axis)
    initial, last = (max(0, -steps), min(count, count - steps))
    return lax.ppermute(value, axis, [(source, source + steps) for source in range(initial, last)])


def dft_tables(length, sign):
    counter = jnp.arange(length, dtype=jnp.int32)
    phase = (jnp.outer(counter, counter) % length).astype(jnp.float32) * (2.0 * jnp.pi / length)
    scale = 1.0 / jnp.sqrt(jnp.float32(length))
    return (
        (jnp.cos(phase) * scale).astype(jnp.bfloat16),
        (sign * jnp.sin(phase) * scale).astype(jnp.bfloat16),
    )


def apply_left(table, wave):
    return jnp.einsum("kn,mnj->mkj", table, wave, preferred_element_type=jnp.float32)


def apply_right(wave, table):
    return jnp.einsum("mkn,nj->mkj", wave, table, preferred_element_type=jnp.float32)


def transform(wave_real, wave_imag, table_real, table_imag):
    mid_real = (apply_left(table_real, wave_real) - apply_left(table_imag, wave_imag)).astype(
        jnp.bfloat16
    )
    mid_imag = (apply_left(table_real, wave_imag) + apply_left(table_imag, wave_real)).astype(
        jnp.bfloat16
    )
    out_real = apply_right(mid_real, table_real) - apply_right(mid_imag, table_imag)
    out_imag = apply_right(mid_real, table_imag) + apply_right(mid_imag, table_real)
    return (out_real, out_imag)


def on_device(object_tile, probe, amplitudes, row_offsets, col_offsets, scan_count):
    side = probe.shape[2]
    width = object_tile.shape[2]
    scans_here = amplitudes.shape[0]
    fwd_real, fwd_imag = dft_tables(side, -1.0)
    inv_real, inv_imag = dft_tables(side, 1.0)
    border = passed_along(object_tile, "tile", -1)
    extended = jnp.concatenate([object_tile, border], axis=2)
    probe_real = probe[:, 0]
    probe_imag = probe[:, 1]
    zero = jnp.int32(0)

    def forward(offsets):
        top, start = offsets
        window = lax.dynamic_slice(extended, (zero, top, start), (2, side, side))
        psi_real = (probe_real * window[0] - probe_imag * window[1]).astype(jnp.bfloat16)
        psi_imag = (probe_real * window[1] + probe_imag * window[0]).astype(jnp.bfloat16)
        spec_real, spec_imag = transform(psi_real, psi_imag, fwd_real, fwd_imag)
        spec_real = spec_real.astype(jnp.bfloat16)
        spec_imag = spec_imag.astype(jnp.bfloat16)
        wide_real = spec_real.astype(jnp.float32)
        wide_imag = spec_imag.astype(jnp.float32)
        partial_power = jnp.sum(wide_real * wide_real + wide_imag * wide_imag, axis=0)
        return (spec_real, spec_imag, partial_power)

    spectra_real, spectra_imag, partial_power = lax.map(forward, (row_offsets, col_offsets))
    intensity = lax.psum(partial_power, "mode")
    activity = (jnp.arange(scans_here, dtype=jnp.int32) < scan_count[0]).astype(jnp.float32)

    def backward(carry, items):
        grid_sum, probe_sum = carry
        spec_real, spec_imag, power, measured, top, start, active = items
        factor = measured / jnp.maximum(jnp.sqrt(power), 0.5) - 1.0
        change_real = (spec_real.astype(jnp.float32) * factor).astype(jnp.bfloat16)
        change_imag = (spec_imag.astype(jnp.float32) * factor).astype(jnp.bfloat16)
        chi_real, chi_imag = transform(change_real, change_imag, inv_real, inv_imag)
        window = lax.dynamic_slice(extended, (zero, top, start), (2, side, side))
        grad_real = jnp.sum(probe_real * chi_real + probe_imag * chi_imag, axis=0)
        grad_imag = jnp.sum(probe_real * chi_imag - probe_imag * chi_real, axis=0)
        update = active * jnp.stack([grad_real, grad_imag])
        current = lax.dynamic_slice(grid_sum, (zero, top, start), (2, side, side))
        grid_sum = lax.dynamic_update_slice(grid_sum, current + update, (zero, top, start))
        pgrad_real = window[0] * chi_real + window[1] * chi_imag
        pgrad_imag = window[0] * chi_imag - window[1] * chi_real
        probe_sum = probe_sum + active * jnp.stack([pgrad_real, pgrad_imag], axis=1)
        return ((grid_sum, probe_sum), None)

    start_grid = jnp.zeros(extended.shape, jnp.float32)
    start_probe = jnp.zeros(probe.shape, jnp.float32)
    items = (spectra_real, spectra_imag, intensity, amplitudes, row_offsets, col_offsets, activity)
    (grid_sum, probe_sum), unused = lax.scan(backward, (start_grid, start_probe), items)
    summed = lax.psum(grid_sum, "mode")
    arriving = passed_along(summed[:, :, width:], "tile", 1)
    total = summed[:, :, :width].at[:, :, :side].add(arriving)
    probe_total = lax.psum(probe_sum, "tile")
    object_new = object_tile + total
    probe_new = probe + probe_total / scans_here
    return (object_new, probe_new)


def solution(mesh):
    in_specs = (
        P(None, None, "tile"),
        P("mode", None, None, None),
        P("tile", None, None),
        P("tile"),
        P("tile"),
        P("tile"),
    )
    out_specs = (P(None, None, "tile"), P("mode", None, None, None))
    return jax.shard_map(
        on_device, mesh=mesh, in_specs=in_specs, out_specs=out_specs, check_vma=False
    )
```

profile of v0, /device:TPU:1, one launch (start us, length us, event | category | flops | bytes accessed | tf_op | source)
XLA Modules:
  0.0 439.6 jit_solution(17844932240342093758)
XLA Ops:
  7.2 5.2 %collective-permute-start = (f32[2,384,256]{2,1,0:T(8,128)}, f32[2,384,256]{2,1,0:T(8,128)}, u32[]{:S(2)}, u32[]{:S(2)}) collective-permute-start(f32[2,384,256]{2,1,0:T(8,128)} %param.14), channel_id=1, source_target_pairs={{4,0},{8,4},{12,8},{16,12},{20,16},{24,20},{28,24},{32,28},{36,32}... | collective-permute-start | bytes 2359304 | tf_op jit(solution)/shard_map/ppermute | solution.py:10
  12.4 2.5 slice_bitcast_fusion
  14.9 1.5 copy.19
  16.7 5.4 %collective-permute-done = f32[2,384,256]{2,1,0:T(8,128)} collective-permute-done((f32[2,384,256]{2,1,0:T(8,128)}, f32[2,384,256]{2,1,0:T(8,128)}, u32[]{:S(2)}, u32[]{:S(2)}) %collective-permute-start) | collective-permute-done | bytes 786464 | tf_op jit(solution)/shard_map/ppermute | solution.py:10
  24.5 35.9 %while.34 = (s32[]{:T(128)}, bf16[2,3,256,256]{3,2,1,0:T(8,128)(2,1)}, bf16[2,3,256,256]{3,2,1,0:T(8,128)(2,1)}, f32[2,256,256]{1,2,0:T(8,128)}, s32[2]{0:T(128)...) while((s32[]{:T(128)}, ...), condition=%wide.region_2.3_spmd.clone.clone, body=%wide.region_0.2_spmd.clone.clone.sunk | while | flops 817954816 | bytes 35652012 | solution.py:68
  28.9 1.3 constant_dynamic-slice_fusion.7
  46.9 1.3 constant_dynamic-slice_fusion.7
  61.3 48.4 %all-reduce.4.cloned.1.call-done = f32[2,256,256]{1,2,0:T(8,128)} async-done(((f32[2,256,256]{1,2,0:T(8,128)}), f32[2,256,256]{1,2,0:T(8,128)}) %all-reduce.4.cloned.1.call-update) | async-done | bytes 524304 | tf_op jit(solution)/shard_map/psum | solution.py:69
  111.0 68.8 %while.35 = (s32[]{:T(128)}, f32[2,384,512]{2,1,0:T(8,128)}, f32[3,2,256,256]{3,2,0,1:T(8,128)}, s32[2]{0:T(128)S(1)}, s32[2]{0:T(128)S(1)}, /*index=5*/f32[2]{0...) while((s32[]{:T(128)}, f32[2,384,512]{2,1,0:T(8,128)}, ...), condition=%wide.region_7.8_spmd.clone.clone, body=%wide.region_4.7_spmd.clone.clone.sunk | while | flops 822018048 | bytes 32506244 | solution.py:93
  127.6 1.3 dynamic-slice_bitcast_fusion.3
  130.2 3.7 add_bitcast_fusion.5
  134.5 2.0 fusion.248
  136.6 2.0 fusion.247
  138.6 6.1 %dynamic_update_slice.35 = f32[2,384,512]{2,1,0:T(8,128)} dynamic-update-slice(f32[2,384,512]{2,1,0:T(8,128)} %get-tuple-element.762, f32[2,256,256]{2,1,0:T(8,128)S(1)} %fusion.247, s32[]{:T(128)} %constant.124.clone.1..sunk.1, s32[]{:T(128)S(6)} %select_n.164, s32[]{:T(128)S(6)} %select_n.165) | dynamic-update-slice | bytes 1048580 | tf_op jit(solution)/shard_map/while/body/eval_jaxpr/dynamic_update_slice | solution.py:84
  161.2 1.3 dynamic-slice_bitcast_fusion.3
  163.8 3.7 add_bitcast_fusion.5
  168.1 3.4 fusion.248
  171.6 2.0 fusion.247
  173.6 6.3 %dynamic_update_slice.35 = f32[2,384,512]{2,1,0:T(8,128)} dynamic-update-slice(f32[2,384,512]{2,1,0:T(8,128)} %get-tuple-element.762, f32[2,256,256]{2,1,0:T(8,128)S(1)} %fusion.247, s32[]{:T(128)} %constant.124.clone.1..sunk.1, s32[]{:T(128)S(6)} %select_n.164, s32[]{:T(128)S(6)} %select_n.165) | dynamic-update-slice | bytes 1048580 | tf_op jit(solution)/shard_map/while/body/eval_jaxpr/dynamic_update_slice | solution.py:84
  182.5 55.6 %all-reduce.6.cloned.1.call-done = f32[2,384,512]{2,1,0:T(8,128)} async-done(((f32[2,384,512]{2,1,0:T(8,128)}), f32[2,384,512]{2,1,0:T(8,128)}) %all-reduce.6.cloned.1.call-update) | async-done | bytes 1572880 | tf_op jit(solution)/shard_map/psum | solution.py:94
  239.4 4.0 collective-permute-start.1
  243.4 184.6 %all-reduce.8.cloned.1.call-done = f32[3,2,256,256]{3,2,1,0:T(8,128)} async-done(((f32[3,2,256,256]{3,2,1,0:T(8,128)}), f32[3,2,256,256]{3,2,1,0:T(8,128)}) %all-reduce.8.cloned.1.call-update) | async-done | bytes 1572880 | tf_op jit(solution)/shard_map/psum | solution.py:97
  427.9 2.9 multiply_add_fusion
  430.8 2.2 fusion.146
  (130 shorter events, 62.9 us)
Async XLA Ops:
  7.2 102.5 %all-reduce.4.cloned.1.call-start = ((), (), s32[]{:S(2)}) async-start(), calls=%async_computation | async-start | bytes 1048576 | tf_op jit(solution)/shard_map/psum | solution.py:69
  7.2 14.9 %collective-permute-start = (f32[2,384,256]{2,1,0:T(8,128)}, f32[2,384,256]{2,1,0:T(8,128)}, u32[]{:S(2)}, u32[]{:S(2)}) collective-permute-start(f32[2,384,256]{2,1,0:T(8,128)} %param.14), channel_id=1, source_target_pairs={{4,0},{8,4},{12,8},{16,12},{20,16},{24,20},{28,24},{32,28},{36,32}... | collective-permute-start | bytes 2359304 | tf_op jit(solution)/shard_map/ppermute | solution.py:10
  14.9 1.8 copy-start.9
  16.6 7.9 %copy-start.14 = (s32[2]{0:T(128)S(1)}, s32[2]{0:T(128)}, u32[]{:S(2)}) copy-start(s32[2]{0:T(128)} %param.17) | copy-start | bytes 28
  16.6 7.9 %copy-start.15 = (s32[2]{0:T(128)S(1)}, s32[2]{0:T(128)}, u32[]{:S(2)}) copy-start(s32[2]{0:T(128)} %param.18) | copy-start | bytes 28
  34.4 2.5 copy-start.7
  36.9 2.5 copy-start.5
  38.1 2.5 copy-start.8
  39.4 2.3 copy-start.12
  52.3 2.5 copy-start.7
  54.8 2.5 copy-start.5
  56.0 2.5 copy-start.8
  57.3 2.3 copy-start.12
  60.4 177.7 %all-reduce.6.cloned.1.call-start = ((), (), s32[]{:S(2)}) async-start(), calls=%async_computation.1 | async-start | bytes 3145728 | tf_op jit(solution)/shard_map/psum | solution.py:94
  134.5 2.0 copy-start.1
  134.5 2.0 copy-start.2
  168.1 3.4 copy-start.1
  168.1 3.4 copy-start.2
  179.8 1.4 copy-start
  179.9 248.1 %all-reduce.8.cloned.1.call-start = ((), (), s32[]{:S(2)}) async-start(), calls=%async_computation.2 | async-start | bytes 3145728 | tf_op jit(solution)/shard_map/psum | solution.py:97
  182.5 245.4 %copy-start.4 = (f32[3,2,256,256]{3,2,1,0:T(8,128)S(1)}, f32[3,2,256,256]{3,2,1,0:T(8,128)}, u32[]{:S(2)}) copy-start(f32[3,2,256,256]{3,2,1,0:T(8,128)} %param.15) | copy-start | bytes 4718596
  239.4 191.5 %copy-start.10 = (f32[2,384,256]{2,1,0:T(8,128)S(1)}, f32[2,384,256]{2,1,0:T(8,128)}, u32[]{:S(2)}) copy-start(f32[2,384,256]{2,1,0:T(8,128)} %param.14) | copy-start | bytes 2359300
  239.4 191.5 %collective-permute-start.1 = (f32[2,384,256]{2,1,0:T(8,128)S(1)}, f32[2,384,256]{2,1,0:T(8,128)}, u32[]{:S(2)}, u32[]{:S(2)}) collective-permute-start(f32[2,384,256]{2,1,0:T(8,128)S(1)} %slice.66), channel_id=1, source_target_pairs={{0,4},{4,8},{8,12},{12,16},{16,20},{20,24},{24,28},{28,32},{32,36}... | collective-permute-start | bytes 2359304 | tf_op jit(solution)/shard_map/ppermute | solution.py:10
  427.9 2.9 copy-start.11
  (5 other events, 4.5 us)
Sparse Core Ops, SparseCore 0:
  60.6 49.1 all-reduce.3
  180.0 58.1 all-reduce.5
  241.6 186.3 all-reduce.7
where the time goes:
time: 442 us; the launch traced here: 440 us
  waiting for transfers between devices  294 us (67%)
  local copies, waits for them, and re-layouts  44.7 us (10%)
  matrix products  44.1 us (10%)
  other arithmetic  17.4 us (4%)
  loops' own time  15.4 us (3%)
  between operations  14.5 us (3%)
  starting transfers between devices  9.47 us (2%)
    psum x1, waiting for transfers between devices, on_device(): probe_total = lax.psum(probe_sum, 'tile')  185 us
    psum x1, waiting for transfers between devices, on_device(): summed = lax.psum(grid_sum, 'mode')  55.6 us
    psum x1, waiting for transfers between devices, on_device(): intensity = lax.psum(partial_power, 'mode')  48.4 us
    dot_general x16, matrix products, apply_right(): jnp.einsum('mkn,nj->mkj', wave, table, preferred_element_type=jnp.float32)  24.6 us
    dot_general x16, matrix products, apply_left(): jnp.einsum('kn,mnj->mkj', table, wave, preferred_element_type=jnp.float32)  19.5 us
    dynamic_update_slice x2, local copies, waits for them, and re-layouts, backward(): lax.dynamic_update_slice(grid_sum, current + update, (zero, top, start))  12.4 us
    ppermute x2, starting transfers between devices, passed_along(): lax.ppermute(value, axis, [(source, source + steps) for source in range(i...  9.17 us
  transfers between devices with their start and end apart: 5, of which 4 were waited for; matrix products, arithmetic and copies ran while one was open for 2% of the time, Pallas kernels for 0%

commit v1 on v0

v1 whole, which is shorter than its diff:
```python
import functools

import jax
import jax.numpy as jnp
import numpy as np
from jax import lax
from jax.experimental import pallas as pl
from jax.experimental.pallas import tpu as pltpu
from jax.sharding import PartitionSpec as P

SIDE = 256
ROWS = 384
MODES = 3
SCANS = 2
NX, NZ, NY = 4, 8, 4
N_TILE = 64
F32 = jnp.float32
BF16 = jnp.bfloat16
BLK = 32


def dft_blocks():
    counter = np.arange(SIDE)
    phase = (np.outer(counter, counter) % SIDE) * (2.0 * np.pi / SIDE)
    real = np.cos(phase) / np.sqrt(SIDE)
    imag = -np.sin(phase) / np.sqrt(SIDE)
    left = np.block([[real, -imag], [imag, real]])
    right = np.block([[real, imag], [-imag, real]])
    return left.astype(np.float32).astype(jnp.bfloat16), right.astype(np.float32).astype(jnp.bfloat16)


class Sems:
    def __init__(self, send, recv):
        self.send, self.recv, self.used, self.started = send, recv, 0, []

    def start(self, src, dst, dev):
        i = self.used
        self.used += 1
        copy = pltpu.make_async_remote_copy(
            src_ref=src,
            dst_ref=dst,
            send_sem=self.send.at[i],
            recv_sem=self.recv.at[i],
            device_id=dev,
            device_id_type=pl.DeviceIdType.MESH,
        )
        copy.start()
        self.started.append(copy)
        return copy


N_SEMS = 64


def rows(start, size):
    return pl.ds(pl.multiple_of(start, 8), size)


def aligned(first):
    base = jnp.minimum(first // 8, 15)
    return base, (BLK + 8 - (first - base * 8)) % (BLK + 8)


def kernel(
    where_ref, active_ref, obj_ref, probe_ref, amp_ref, lf_ref, rf_ref,
    onew_ref, pnew_ref,
    border, win, psi, half, spec, power, pw_a, pw_b, factor, pad, pgrad, p_core,
    px1, px2, pz, own, edge, ro1, ro2, re1, re2, arrive,
    send_sem, recv_sem,
):
    t = lax.axis_index("tile")
    y = lax.axis_index("mode")
    core = t % 2
    z = (t // 2) % NZ
    x = t // (2 * NZ)
    sems = Sems(send_sem, recv_sem)

    def tile_dev(xx, zz, cc):
        return ((xx * NZ + zz) * 2 + cc, y)

    t_left = ((t + N_TILE - 1) % N_TILE, y)
    t_right = ((t + 1) % N_TILE, y)
    peer = tile_dev(x, z, 1 - core)

    def pairs(i):
        return (i + 1 - 2 * (i % 2), 3 - i, ((i + 1) // 2) % 2, i // 2)

    ya, yb, yha, yhb = pairs(y)
    xa, xb, xha, xhb = pairs(x)
    y_dev = ((t, ya), (t, yb))
    x_dev = (tile_dev(xa, z, core), tile_dev(xb, z, core))
    y_half = (yha, yhb)
    x_half = (xha, xhb)
    z_dev = [tile_dev(x, (z + k) % NZ, core) for k in range(1, NZ)]

    barrier = pltpu.get_barrier_semaphore()
    partners = [t_left, t_right, *y_dev, *x_dev, *z_dev]
    for dev in partners:
        pl.semaphore_signal(barrier, inc=1, device_id=dev, device_id_type=pl.DeviceIdType.MESH)
    pl.semaphore_wait(barrier, len(partners))

    get_border = sems.start(obj_ref, border, t_left)
    for s in range(SCANS):
        for c in range(2):
            pad[s, c, 0:16] = jnp.zeros((16, 8, SIDE), F32)
            pad[s, c, 48:64] = jnp.zeros((16, 8, SIDE), F32)
    get_border.wait_recv()

    @pl.when(t == N_TILE - 1)
    def _():
        border[...] = jnp.zeros(border.shape, F32)

    def forward(s):
        base, up, shift = where_ref[0, s], where_ref[1, s], where_ref[4, s]

        def cut(i, carry):
            for c in range(2):
                at = pl.ds(base + i * (BLK // 8), BLK // 8 + 1)
                wide = jnp.concatenate([obj_ref[c, at], border[c, at]], axis=2).reshape(BLK + 8, 2 * SIDE)
                wide = pltpu.roll(wide, up, axis=0)[:BLK]
                win[s, c, rows(i * BLK, BLK), :] = pltpu.roll(wide, shift, axis=1)[:, :SIDE]
            return carry

        lax.fori_loop(0, SIDE // BLK, cut, 0)

        def mode(m, carry):
            pr = probe_ref[rows(m * 2 * SIDE, SIDE), :]
            pi = probe_ref[rows(m * 2 * SIDE + SIDE, SIDE), :]
            wr, wi = win[s, 0], win[s, 1]
            psi[0:SIDE, :] = (pr * wr - pi * wi).astype(BF16)
            psi[SIDE:, :] = (pr * wi + pi * wr).astype(BF16)
            mid = jnp.dot(lf_ref[...], psi[...], preferred_element_type=F32).astype(BF16)
            half[:, 0:SIDE] = mid[0:SIDE]
            half[:, SIDE:] = mid[SIDE:]
            out = jnp.dot(half[...], rf_ref[...], preferred_element_type=F32).astype(BF16)
            spec[s, m] = out
            wide = out.astype(F32)
            wide = wide * wide
            power[s] = jnp.where(m == 0, 0.0, power[s]) + wide[:, :SIDE] + wide[:, SIDE:]
            return carry

        lax.fori_loop(0, MODES, mode, 0)

    def order(s):
        return (s, 1 - s)

    step1, step2 = [], []
    for s in range(SCANS):
        forward(s)
        first, _ = order(s)
        h = y_half[first]
        step1.append(sems.start(power.at[s, rows((1 - h) * 128, 128), :], pw_a.at[s], y_dev[first]))
    quarter = []
    for s in range(SCANS):
        first, second = order(s)
        h, g = y_half[first], y_half[second]
        base = h * 128
        step1[s].wait_recv()
        power[s, rows(base, 128), :] = power[s, rows(base, 128), :] + pw_a[s]
        step2.append(sems.start(power.at[s, rows(base + (1 - g) * 64, 64), :], pw_b.at[s], y_dev[second]))
        quarter.append(base + g * 64)
    gather1, gather2 = [], []
    for s in range(SCANS):
        first, second = order(s)
        q = rows(quarter[s], 64)
        step2[s].wait_recv()
        total = power[s, q, :] + pw_b[s]
        factor[s, q, :] = amp_ref[s, q, :] / jnp.maximum(jnp.sqrt(total), 0.5) - 1.0
        gather1.append(sems.start(factor.at[s, q, :], factor.at[s, q, :], y_dev[second]))
    for s in range(SCANS):
        first, second = order(s)
        q = rows(y_half[first] * 128, 128)
        gather1[s].wait_recv()
        gather2.append(sems.start(factor.at[s, q, :], factor.at[s, q, :], y_dev[first]))

    def backward(s):
        active = active_ref[s]

        def mode(m, carry):
            f = factor[s]
            psi[0:SIDE, :] = (spec[s, m, :, :SIDE].astype(F32) * f).astype(BF16)
            psi[SIDE:, :] = (spec[s, m, :, SIDE:].astype(F32) * f).astype(BF16)
            mid = jnp.dot(rf_ref[...], psi[...], preferred_element_type=F32).astype(BF16)
            half[:, 0:SIDE] = mid[0:SIDE]
            half[:, SIDE:] = mid[SIDE:]
            chi = jnp.dot(half[...], lf_ref[...], preferred_element_type=F32) * active
            cr, ci = chi[:, :SIDE], chi[:, SIDE:]
            at_r, at_i = rows(m * 2 * SIDE, SIDE), rows(m * 2 * SIDE + SIDE, SIDE)
            pr, pi = probe_ref[at_r, :], probe_ref[at_i, :]
            wr, wi = win[s, 0], win[s, 1]
            gr = (pr * cr + pi * ci).reshape(SIDE // 8, 8, SIDE)
            gi = (pr * ci - pi * cr).reshape(SIDE // 8, 8, SIDE)
            pad[s, 0, 16:48] = jnp.where(m == 0, 0.0, pad[s, 0, 16:48]) + gr
            pad[s, 1, 16:48] = jnp.where(m == 0, 0.0, pad[s, 1, 16:48]) + gi
            if s == 0:
                pgrad[at_r, :] = wr * cr + wi * ci
                pgrad[at_i, :] = wr * ci - wi * cr
            else:
                pgrad[at_r, :] = pgrad[at_r, :] + wr * cr + wi * ci
                pgrad[at_i, :] = pgrad[at_i, :] + wr * ci - wi * cr
            return carry

        lax.fori_loop(0, MODES, mode, 0)

    for s in range(SCANS):
        gather2[s].wait_recv()
        backward(s)

    n_core = MODES * SIDE
    mine = core * n_core
    core_copy = sems.start(pgrad.at[rows((1 - core) * n_core, n_core), :], p_core, peer)

    def place(i, carry):
        for c in range(2):
            total = None
            for s in range(SCANS):
                base, up = where_ref[2, s], where_ref[3, s]
                block = pad[s, c, pl.ds(base + i * (BLK // 8), BLK // 8 + 1)].reshape(BLK + 8, SIDE)
                block = pltpu.roll(block, up, axis=0)[:BLK]
                wide = jnp.concatenate([block, jnp.zeros((BLK, SIDE), F32)], axis=1)
                wide = pltpu.roll(wide, where_ref[5, s], axis=1)
                total = wide if total is None else total + wide
            own[c, rows(i * BLK, BLK), :] = total[:, :SIDE]
            edge[c, rows(i * BLK, BLK), :] = total[:, SIDE:]
        return carry

    lax.fori_loop(0, ROWS // BLK, place, 0)

    half_rows, quarter_rows = ROWS // 2, ROWS // 4

    def reduce_1(grid, landing):
        copies = []
        for c in range(2):
            h = y_half[order(c)[0]]
            copies.append(
                sems.start(grid.at[c, rows((1 - h) * half_rows, half_rows), :], landing.at[c], y_dev[order(c)[0]])
            )
        return copies

    def reduce_2(grid, landing_1, landing_2, copies):
        result = []
        for c in range(2):
            first, second = order(c)
            h, g = y_half[first], y_half[second]
            base = h * half_rows
            copies[c].wait_recv()
            grid[c, rows(base, half_rows), :] = grid[c, rows(base, half_rows), :] + landing_1[c]
            result.append(
                sems.start(
                    grid.at[c, rows(base + (1 - g) * quarter_rows, quarter_rows), :], landing_2.at[c], y_dev[second]
                )
            )
        return result

    def quarter_at(c):
        first, second = order(c)
        return y_half[first] * half_rows + y_half[second] * quarter_rows

    def quarter_of(c):
        return rows(quarter_at(c), quarter_rows)

    edge_1 = reduce_1(edge, re1)
    own_1 = reduce_1(own, ro1)

    core_copy.wait_recv()
    pgrad[rows(mine, n_core), :] = pgrad[rows(mine, n_core), :] + p_core[...]
    n_part, n_half, n_quarter = n_core // 2, n_core // 4, n_core // 8
    x_1 = []
    for k in range(2):
        first, _ = order(k)
        x_1.append(
            sems.start(
                pgrad.at[rows(mine + k * n_part + (1 - x_half[first]) * n_half, n_half), :], px1.at[k], x_dev[first]
            )
        )

    edge_2 = reduce_2(edge, re1, re2, edge_1)

    x_2, x_at = [], []
    for k in range(2):
        first, second = order(k)
        base = mine + k * n_part + x_half[first] * n_half
        x_1[k].wait_recv()
        pgrad[rows(base, n_half), :] = pgrad[rows(base, n_half), :] + px1[k]
        x_2.append(
            sems.start(pgrad.at[rows(base + (1 - x_half[second]) * n_quarter, n_quarter), :], px2.at[k], x_dev[second])
        )
        x_at.append(base + x_half[second] * n_quarter)

    own_2 = reduce_2(own, ro1, ro2, own_1)

    cross = []
    for c in range(2):
        edge_2[c].wait_recv()
        edge[c, quarter_of(c), :] = edge[c, quarter_of(c), :] + re2[c]
        cross.append(sems.start(edge.at[c, quarter_of(c), :], arrive.at[c], t_right))

    for k in range(2):
        x_2[k].wait_recv()
        pgrad[rows(x_at[k], n_quarter), :] = pgrad[rows(x_at[k], n_quarter), :] + px2[k]

    n_z = 2 * n_quarter // NZ

    def z_rows(zz):
        return rows(x_at[0] + (zz // 4) * (x_at[1] - x_at[0]) + (zz % 4) * n_z, n_z)

    z_copies = []
    for k in range(1, NZ):
        z_copies.append(sems.start(pgrad.at[z_rows((z + k) % NZ), :], pz.at[k - 1], z_dev[k - 1]))

    gather_1 = []
    for c in range(2):
        own_2[c].wait_recv()
        cross[c].wait_recv()
        q = quarter_of(c)
        q8 = pl.ds(quarter_at(c) // 8, quarter_rows // 8)
        mine_now = obj_ref[c, q8].reshape(quarter_rows, SIDE)
        onew_ref[c, q, :] = mine_now + own[c, q, :] + ro2[c] + jnp.where(t == 0, 0.0, arrive[c])
        gather_1.append(sems.start(onew_ref.at[c, q, :], onew_ref.at[c, q, :], y_dev[order(c)[1]]))

    total = pgrad[z_rows(z), :]
    for k in range(1, NZ):
        z_copies[k - 1].wait_recv()
        total = total + pz[k - 1]
    pnew_ref[z_rows(z), :] = probe_ref[z_rows(z), :] + total * 0.5
    z_gather = []
    for k in range(1, NZ):
        z_gather.append(sems.start(pnew_ref.at[z_rows(z), :], pnew_ref.at[z_rows(z), :], z_dev[k - 1]))

    gather_2 = []
    for c in range(2):
        gather_1[c].wait_recv()
        q = rows(y_half[order(c)[0]] * half_rows, half_rows)
        gather_2.append(sems.start(onew_ref.at[c, q, :], onew_ref.at[c, q, :], y_dev[order(c)[0]]))

    for copy in z_gather:
        copy.wait_recv()
    x_g1, x_g2 = [], []
    for k in range(2):
        at = rows(x_at[k], n_quarter)
        x_g1.append(sems.start(pnew_ref.at[at, :], pnew_ref.at[at, :], x_dev[order(k)[1]]))
    for k in range(2):
        x_g1[k].wait_recv()
        at = rows(mine + k * n_part + x_half[order(k)[0]] * n_half, n_half)
        x_g2.append(sems.start(pnew_ref.at[at, :], pnew_ref.at[at, :], x_dev[order(k)[0]]))
    for k in range(2):
        x_g2[k].wait_recv()
    last = sems.start(pnew_ref.at[rows(mine, n_core), :], pnew_ref.at[rows(mine, n_core), :], peer)
    for c in range(2):
        gather_2[c].wait_recv()
    last.wait_recv()
    for copy in sems.started:
        copy.wait_send()


def on_device(object_tile, probe, amplitudes, row_offsets, col_offsets, scan_count):
    left, right = dft_blocks()
    vmem = pl.BlockSpec(memory_space=pltpu.VMEM)
    smem = pl.BlockSpec(memory_space=pltpu.SMEM)
    n = 2 * MODES * SIDE
    flat = probe.reshape(n, SIDE)
    places = jnp.stack(
        [
            *aligned(row_offsets),
            *aligned(ROWS - SIDE - row_offsets),
            (2 * SIDE - col_offsets) % (2 * SIDE),
            col_offsets,
        ]
    )
    active = (jnp.arange(SCANS, dtype=jnp.int32) < scan_count[0]).astype(F32)
    scratch = [
        pltpu.VMEM((2, ROWS // 8, 8, SIDE), F32),
        pltpu.VMEM((SCANS, 2, SIDE, SIDE), F32),
        pltpu.VMEM((2 * SIDE, SIDE), BF16),
        pltpu.VMEM((SIDE, 2 * SIDE), BF16),
        pltpu.VMEM((SCANS, MODES, SIDE, 2 * SIDE), BF16),
        pltpu.VMEM((SCANS, SIDE, SIDE), F32),
        pltpu.VMEM((SCANS, SIDE // 2, SIDE), F32),
        pltpu.VMEM((SCANS, SIDE // 4, SIDE), F32),
        pltpu.VMEM((SCANS, SIDE, SIDE), F32),
        pltpu.VMEM((SCANS, 2, 2 * SIDE // 8, 8, SIDE), F32),
        pltpu.VMEM((n, SIDE), F32),
        pltpu.VMEM((n // 2, SIDE), F32),
        pltpu.VMEM((2, n // 8, SIDE), F32),
        pltpu.VMEM((2, n // 16, SIDE), F32),
        pltpu.VMEM((NZ - 1, n // 64, SIDE), F32),
        pltpu.VMEM((2, ROWS, SIDE), F32),
        pltpu.VMEM((2, ROWS, SIDE), F32),
        pltpu.VMEM((2, ROWS // 2, SIDE), F32),
        pltpu.VMEM((2, ROWS // 4, SIDE), F32),
        pltpu.VMEM((2, ROWS // 2, SIDE), F32),
        pltpu.VMEM((2, ROWS // 4, SIDE), F32),
        pltpu.VMEM((2, ROWS // 4, SIDE), F32),
        pltpu.SemaphoreType.DMA((N_SEMS,)),
        pltpu.SemaphoreType.DMA((N_SEMS,)),
    ]
    object_new, probe_new = pl.pallas_call(
        kernel,
        out_shape=(
            jax.ShapeDtypeStruct(object_tile.shape, F32),
            jax.ShapeDtypeStruct(flat.shape, F32),
        ),
        in_specs=[smem, smem, vmem, vmem, vmem, vmem, vmem],
        out_specs=(vmem, vmem),
        scratch_shapes=scratch,
        compiler_params=pltpu.CompilerParams(
            collective_id=0, has_side_effects=True, vmem_limit_bytes=56 * 1024 * 1024
        ),
        cost_estimate=pl.CostEstimate(flops=3_300_000_000, bytes_accessed=6_000_000, transcendentals=131072),
    )(places, active, object_tile.reshape(2, ROWS // 8, 8, SIDE), flat, amplitudes, jnp.asarray(left), jnp.asarray(right))
    return object_new, probe_new.reshape(probe.shape)


def solution(mesh):
    in_specs = (
        P(None, None, "tile"),
        P("mode", None, None, None),
        P("tile", None, None),
        P("tile"),
        P("tile"),
        P("tile"),
    )
    out_specs = (P(None, None, "tile"), P("mode", None, None, None))
    return jax.shard_map(on_device, mesh=mesh, in_specs=in_specs, out_specs=out_specs, check_vma=False)
```

time: 442 us -> 96.5 us (0.22)
  waiting for transfers between devices: 294 us -> 0 us
  Pallas kernels: 0 us -> 88.6 us
  matrix products: 44.1 us -> 0 us
  local copies, waits for them, and re-layouts: 44.7 us -> 4.59 us
  other arithmetic: 17.4 us -> 1.86 us
  loops' own time: 15.4 us -> 0 us
  between operations: 14.5 us -> 1.29 us
  starting transfers between devices: 9.47 us -> 0 us
    psum x3 -> x0, waiting for transfers between devices: 289 us -> none  [the longest x1 185 us: on_device(): probe_total = lax.psum(probe_sum, 'tile')]
    pallas_call x0 -> x1, Pallas kernels: none -> 88.6 us  [on_device(): pl.pallas_call(kernel, out_shape=(jax.ShapeDtypeStruct(object_tile.shape,...]
    dot_general x32 -> x0, matrix products: 44.1 us -> none  [the longest x16 24.6 us: apply_right(): jnp.einsum('mkn,nj->mkj', wave, table, preferred_element_type=jnp.float32)]
    another operation x2 -> x0, loops' own time: 15.4 us -> none  [the longest x1 8.47 us: on_device(): lax.scan(backward, (start_grid, start_probe), items)]
    add x6 -> x0, other arithmetic: 14.6 us -> none  [the longest x2 5.47 us: backward(): probe_sum = probe_sum + active * jnp.stack([pgrad_real, pgrad_imag], axis=1)]
    dynamic_update_slice x6 -> x0, local copies, waits for them, and re-layouts: 12.7 us -> none  [the longest x2 12.4 us: backward(): lax.dynamic_update_slice(grid_sum, current + update, (zero, top, start))]
    dynamic_slice x20 -> x0, local copies, waits for them, and re-layouts: 11.3 us -> none  [the longest x12 6.45 us: on_device(): lax.scan(backward, (start_grid, start_probe), items)]
    ppermute x2 -> x0, starting transfers between devices: 9.17 us -> none  [passed_along(): lax.ppermute(value, axis, [(source, source + steps) for source in range(i...]
  transfers between devices with their start and end apart: 5 -> 0, of which waited for: 4 -> 0; matrix products, arithmetic and copies ran while one was open for 2% -> 0% of each run, Pallas kernels for 0% -> 0%
where the time goes in v1:
time: 96.5 us; the launch traced here: 96.3 us
  Pallas kernels  88.6 us (92%)
  local copies, waits for them, and re-layouts  4.59 us (5%)
  other arithmetic  1.86 us (2%)
  between operations  1.29 us (1%)
    pallas_call x1, Pallas kernels, on_device(): pl.pallas_call(kernel, out_shape=(jax.ShapeDtypeStruct(object_tile.shape,...  88.6 us
    unnamed x4, local copies, waits for them, and re-layouts  3.33 us

profile of v1, /device:TPU:1, one launch (start us, length us, event | category | flops | bytes accessed | tf_op | source)
XLA Modules:
  0.0 96.3 jit_solution(16947608598139073406)
XLA Ops:
  1.3 0.5 compare_convert_fusion.active_ref
  1.8 0.7 fusion.2
  2.5 0.7 fusion.1
  3.1 1.3 %stack.27.where_ref = s32[6,2]{1,0:T(8,128)} concatenate(s32[1,2]{1,0:T(1,128)S(1)} %bitcast.16, s32[1,2]{1,0:T(1,128)S(1)} %get-tuple-element.10, s32[1,2]{1,0:T(1,128)S(1)} %bitcast.15, s32[1,2]{1,0:T(1,128)S(1)} %get-tuple-element.6, s32[1,2]{1,0:T(1,128)S(1)} %fusion.2, s32[1,2]{1,0:T(1,128)} %bitcast.17), dimensions={0} | concatenate | bytes 96 | tf_op jit(solution)/shard_map/stack | solution.py:362
  4.4 88.6 %shard_map.95 = (f32[2,384,256]{2,1,0:T(8,128)}, f32[1536,256]{1,0:T(8,128)}) custom-call(s32[6,2]{1,0:T(8,128)} %stack.27.where_ref, f32[2]{0:T(128)} %compare_convert_fusion.active_ref, f32[2,48,8,256]{3,2,1,0:T(8,128)} %bitcast.19, f32[1536,256]{1,0:T(8,128)} %bitcast.18, f32[2,256,256]{2,1,0:T(8,128)} %amp_ref.1, ...), custom_call_target="tpu_custom_call" | custom-call | flops 3300000000 | bytes 6000000 | tf_op jit(solution)/shard_map/pallas_call | solution.py:397
  93.0 0.0 copy-start
  93.0 2.2 %copy.20 = f32[2,384,256]{2,1,0:T(8,128)} copy(f32[2,384,256]{2,1,0:T(8,128)} %get-tuple-element.14) | data formatting | bytes 1572864
  95.2 0.0 copy-done
  95.2 1.1 %copy.21 = f32[3,2,256,256]{3,2,1,0:T(8,128)} copy(f32[3,2,256,256]{3,2,1,0:T(8,128)S(1)} %bitcast.14) | data formatting | bytes 3145728
Async XLA Ops:
  93.0 2.2 %copy-start = (f32[1536,256]{1,0:T(8,128)S(1)}, f32[1536,256]{1,0:T(8,128)}, u32[]{:S(2)}) copy-start(f32[1536,256]{1,0:T(8,128)} %get-tuple-element.5) | copy-start | bytes 4718596

commit v2 on v1

--- a/solution.py
+++ b/solution.py
@@ -33,7 +33,7 @@
     def __init__(self, send, recv):
         self.send, self.recv, self.used, self.started = send, recv, 0, []
 
-    def start(self, src, dst, dev):
+    def make(self, src, dst, dev):
         i = self.used
         self.used += 1
         copy = pltpu.make_async_remote_copy(
@@ -44,6 +44,10 @@
             device_id=dev,
             device_id_type=pl.DeviceIdType.MESH,
         )
+        return copy
+
+    def start(self, src, dst, dev):
+        copy = self.make(src, dst, dev)
         copy.start()
         self.started.append(copy)
         return copy
@@ -56,17 +60,19 @@
     return pl.ds(pl.multiple_of(start, 8), size)
 
 
-def aligned(first):
-    base = jnp.minimum(first // 8, 15)
-    return base, (BLK + 8 - (first - base * 8)) % (BLK + 8)
+def shifted(blocks, rest):
+    turned = pltpu.roll(blocks, (16 - rest) % 8, axis=1)
+    row = lax.broadcasted_iota(jnp.int32, turned[1:].shape, 1)
+    return jnp.where(row < 8 - rest, turned[:-1], turned[1:])
 
 
 def kernel(
-    where_ref, active_ref, obj_ref, probe_ref, amp_ref, lf_ref, rf_ref,
+    row_ref, col_ref, cnt_ref, obj_hbm, probe_hbm, amp_hbm, lf_hbm, rf_hbm,
     onew_ref, pnew_ref,
+    obj, probe_ref, amp_ref, lf_ref, rf_ref,
     border, win, psi, half, spec, power, pw_a, pw_b, factor, pad, pgrad, p_core,
     px1, px2, pz, own, edge, ro1, ro2, re1, re2, arrive,
-    send_sem, recv_sem,
+    send_sem, recv_sem, fetch_sem,
 ):
     t = lax.axis_index("tile")
     y = lax.axis_index("mode")
@@ -93,32 +99,73 @@
     x_half = (xha, xhb)
     z_dev = [tile_dev(x, (z + k) % NZ, core) for k in range(1, NZ)]
 
+    fetch = []
+    for src, dst in ((obj_hbm, obj), (probe_hbm, probe_ref), (lf_hbm, lf_ref), (rf_hbm, rf_ref), (amp_hbm, amp_ref)):
+        fetch.append(pltpu.make_async_copy(src, dst, fetch_sem.at[len(fetch)]))
+        fetch[-1].start()
+
     barrier = pltpu.get_barrier_semaphore()
     partners = [t_left, t_right, *y_dev, *x_dev, *z_dev]
     for dev in partners:
         pl.semaphore_signal(barrier, inc=1, device_id=dev, device_id_type=pl.DeviceIdType.MESH)
     pl.semaphore_wait(barrier, len(partners))
 
-    get_border = sems.start(obj_ref, border, t_left)
+    quarter_blocks = ROWS // 32
+
+    def border_part(index):
+        return pl.ds(index * quarter_blocks, quarter_blocks)
+
+    def near(part, ref):
+        return ref.at[:, border_part(part)]
+
+    whole = sems.make(obj_hbm, border, peer)
+    direct = [sems.make(near(k, obj_hbm), near(k, border), t_left) for k in (y, (y + 2) % NY)]
+    passed = [sems.make(near(y, border), near(y, border), dev) for dev in y_dev]
+
+    @pl.when(core == 1)
+    def _():
+        whole.start()
+
+    @pl.when(core == 0)
+    def _():
+        direct[0].start()
+        direct[1].start()
+
     for s in range(SCANS):
         for c in range(2):
             pad[s, c, 0:16] = jnp.zeros((16, 8, SIDE), F32)
             pad[s, c, 48:64] = jnp.zeros((16, 8, SIDE), F32)
-    get_border.wait_recv()
-
-    @pl.when(t == N_TILE - 1)
-    def _():
-        border[...] = jnp.zeros(border.shape, F32)
+
+    for copy in fetch:
+        copy.wait()
+
+    @pl.when(core == 1)
+    def _():
+        direct[0].wait_recv()
+        passed[0].start()
+        passed[1].start()
+        direct[1].wait_recv()
+        passed[0].wait_recv()
+        passed[1].wait_recv()
+
+    @pl.when(core == 0)
+    def _():
+        whole.wait_recv()
+
+    lane = lax.broadcasted_iota(jnp.int32, (BLK // 8 + 1, 8, SIDE), 2)
+    beyond = jnp.where(t == N_TILE - 1, 0.0, 1.0).astype(F32)
 
     def forward(s):
-        base, up, shift = where_ref[0, s], where_ref[1, s], where_ref[4, s]
+        top, col = row_ref[s], col_ref[s]
+        base = jnp.minimum(top // 8, 15)
+        rest = top - base * 8
 
         def cut(i, carry):
+            at = pl.ds(base + i * (BLK // 8), BLK // 8 + 1)
             for c in range(2):
-                at = pl.ds(base + i * (BLK // 8), BLK // 8 + 1)
-                wide = jnp.concatenate([obj_ref[c, at], border[c, at]], axis=2).reshape(BLK + 8, 2 * SIDE)
-                wide = pltpu.roll(wide, up, axis=0)[:BLK]
-                win[s, c, rows(i * BLK, BLK), :] = pltpu.roll(wide, shift, axis=1)[:, :SIDE]
+                block = jnp.where(lane >= col, obj[c, at], border[c, at] * beyond)
+                block = pltpu.roll(shifted(block, rest), (SIDE - col) % SIDE, axis=2)
+                win[s, c, rows(i * BLK, BLK), :] = block.reshape(BLK, SIDE)
             return carry
 
         lax.fori_loop(0, SIDE // BLK, cut, 0)
@@ -174,7 +221,7 @@
         gather2.append(sems.start(factor.at[s, q, :], factor.at[s, q, :], y_dev[first]))
 
     def backward(s):
-        active = active_ref[s]
+        active = jnp.where(s < cnt_ref[0], 1.0, 0.0).astype(F32)
 
         def mode(m, carry):
             f = factor[s]
@@ -212,16 +259,17 @@
 
     def place(i, carry):
         for c in range(2):
-            total = None
+            inside = outside = 0.0
             for s in range(SCANS):
-                base, up = where_ref[2, s], where_ref[3, s]
-                block = pad[s, c, pl.ds(base + i * (BLK // 8), BLK // 8 + 1)].reshape(BLK + 8, SIDE)
-                block = pltpu.roll(block, up, axis=0)[:BLK]
-                wide = jnp.concatenate([block, jnp.zeros((BLK, SIDE), F32)], axis=1)
-                wide = pltpu.roll(wide, where_ref[5, s], axis=1)
-                total = wide if total is None else total + wide
-            own[c, rows(i * BLK, BLK), :] = total[:, :SIDE]
-            edge[c, rows(i * BLK, BLK), :] = total[:, SIDE:]
+                col, down = col_ref[s], 128 - row_ref[s]
+                base = jnp.minimum(down // 8, 15)
+                block = pad[s, c, pl.ds(base + i * (BLK // 8), BLK // 8 + 1)]
+                block = pltpu.roll(shifted(block, down - base * 8), col, axis=2)
+                here = lane[1:] >= col
+                inside = inside + jnp.where(here, block, 0.0)
+                outside = outside + jnp.where(here, 0.0, block)
+            own[c, rows(i * BLK, BLK), :] = inside.reshape(BLK, SIDE)
+            edge[c, rows(i * BLK, BLK), :] = outside.reshape(BLK, SIDE)
         return carry
 
     lax.fori_loop(0, ROWS // BLK, place, 0)
@@ -314,7 +362,7 @@
         cross[c].wait_recv()
         q = quarter_of(c)
         q8 = pl.ds(quarter_at(c) // 8, quarter_rows // 8)
-        mine_now = obj_ref[c, q8].reshape(quarter_rows, SIDE)
+        mine_now = obj[c, q8].reshape(quarter_rows, SIDE)
         onew_ref[c, q, :] = mine_now + own[c, q, :] + ro2[c] + jnp.where(t == 0, 0.0, arrive[c])
         gather_1.append(sems.start(onew_ref.at[c, q, :], onew_ref.at[c, q, :], y_dev[order(c)[1]]))
 
@@ -352,6 +400,16 @@
     for copy in sems.started:
         copy.wait_send()
 
+    @pl.when(core == 1)
+    def _():
+        for copy in (whole, *passed):
+            copy.wait_send()
+
+    @pl.when(core == 0)
+    def _():
+        for copy in direct:
+            copy.wait_send()
+
 
 def on_device(object_tile, probe, amplitudes, row_offsets, col_offsets, scan_count):
     left, right = dft_blocks()
@@ -359,16 +417,13 @@
     smem = pl.BlockSpec(memory_space=pltpu.SMEM)
     n = 2 * MODES * SIDE
     flat = probe.reshape(n, SIDE)
-    places = jnp.stack(
-        [
-            *aligned(row_offsets),
-            *aligned(ROWS - SIDE - row_offsets),
-            (2 * SIDE - col_offsets) % (2 * SIDE),
-            col_offsets,
-        ]
-    )
-    active = (jnp.arange(SCANS, dtype=jnp.int32) < scan_count[0]).astype(F32)
+    anywhere = pl.BlockSpec(memory_space=pl.ANY)
     scratch = [
+        pltpu.VMEM((2, ROWS // 8, 8, SIDE), F32),
+        pltpu.VMEM((n, SIDE), F32),
+        pltpu.VMEM((SCANS, SIDE, SIDE), F32),
+        pltpu.VMEM((2 * SIDE, 2 * SIDE), BF16),
+        pltpu.VMEM((2 * SIDE, 2 * SIDE), BF16),
         pltpu.VMEM((2, ROWS // 8, 8, SIDE), F32),
         pltpu.VMEM((SCANS, 2, SIDE, SIDE), F32),
         pltpu.VMEM((2 * SIDE, SIDE), BF16),
@@ -393,6 +448,7 @@
         pltpu.VMEM((2, ROWS // 4, SIDE), F32),
         pltpu.SemaphoreType.DMA((N_SEMS,)),
         pltpu.SemaphoreType.DMA((N_SEMS,)),
+        pltpu.SemaphoreType.DMA((5,)),
     ]
     object_new, probe_new = pl.pallas_call(
         kernel,
@@ -400,14 +456,23 @@
             jax.ShapeDtypeStruct(object_tile.shape, F32),
             jax.ShapeDtypeStruct(flat.shape, F32),
         ),
-        in_specs=[smem, smem, vmem, vmem, vmem, vmem, vmem],
+        in_specs=[smem] * 3 + [anywhere] * 5,
         out_specs=(vmem, vmem),
         scratch_shapes=scratch,
         compiler_params=pltpu.CompilerParams(
             collective_id=0, has_side_effects=True, vmem_limit_bytes=56 * 1024 * 1024
         ),
         cost_estimate=pl.CostEstimate(flops=3_300_000_000, bytes_accessed=6_000_000, transcendentals=131072),
-    )(places, active, object_tile.reshape(2, ROWS // 8, 8, SIDE), flat, amplitudes, jnp.asarray(left), jnp.asarray(right))
+    )(
+        row_offsets,
+        col_offsets,
+        scan_count,
+        object_tile.reshape(2, ROWS // 8, 8, SIDE),
+        flat,
+        amplitudes,
+        jnp.asarray(left),
+        jnp.asarray(right),
+    )
     return object_new, probe_new.reshape(probe.shape)
 
 

time: 96.5 us -> 89.1 us (0.923)
  Pallas kernels: 88.6 us -> 84.3 us
  other arithmetic: 1.86 us -> 0 us
  local copies, waits for them, and re-layouts: 4.59 us -> 3.33 us
    pallas_call x1, Pallas kernels: 88.6 us -> 84.3 us  [on_device(): pl.pallas_call(kernel, out_shape=(jax.ShapeDtypeStruct(object_tile.shape,...]
    another operation x2 -> x0, other arithmetic: 1.34 us -> none  [on_device(): jnp.stack([*aligned(row_offsets), *aligned(ROWS - SIDE - row_offsets), (2...]
    another operation x1 -> x0, local copies, waits for them, and re-layouts: 1.26 us -> none  [on_device(): jnp.stack([*aligned(row_offsets), *aligned(ROWS - SIDE - row_offsets), (2...]
where the time goes in v2:
time: 89.1 us; the launch traced here: 89 us
  Pallas kernels  84.3 us (95%)
  local copies, waits for them, and re-layouts  3.33 us (4%)
  between operations  1.29 us (1%)
    pallas_call x1, Pallas kernels, on_device(): pl.pallas_call(kernel, out_shape=(jax.ShapeDtypeStruct(object_tile.shape,...  84.3 us
    unnamed x4, local copies, waits for them, and re-layouts  3.33 us

profile of v2, /device:TPU:1, one launch (start us, length us, event | category | flops | bytes accessed | tf_op | source)
XLA Modules:
  0.0 89.0 jit_solution(5713320029714661683)
XLA Ops:
  1.3 84.3 %shard_map.95 = (f32[2,384,256]{2,1,0:T(8,128)}, f32[1536,256]{1,0:T(8,128)}) custom-call(s32[2]{0:T(128)} %row_ref.1, s32[2]{0:T(128)} %col_ref.1, s32[1]{0:T(128)S(6)} %copy.12.cnt_ref, f32[2,48,8,256]{3,2,1,0:T(8,128)} %bitcast.5, f32[1536,256]{1,0:T(8,128)} %bitcast.4, f32[2,256,256]{2,1,0:T(8,128)} %amp_hbm.1, bf16[512,512]{1,0:T(8,128)(2,1)} %constant.4.clone.lf_hbm, ...), custom_call_target="tpu_custom_call" | custom-call | flops 3300000000 | bytes 6000000 | tf_op jit(solution)/shard_map/pallas_call | solution.py:453
  85.6 0.0 copy-start
  85.6 2.2 %copy.13 = f32[2,384,256]{2,1,0:T(8,128)} copy(f32[2,384,256]{2,1,0:T(8,128)} %get-tuple-element.8) | data formatting | bytes 1572864
  87.8 0.0 copy-done
  87.8 1.1 %copy.14 = f32[3,2,256,256]{3,2,1,0:T(8,128)} copy(f32[3,2,256,256]{3,2,1,0:T(8,128)S(1)} %bitcast.3) | data formatting | bytes 3145728
Async XLA Ops:
  85.6 2.2 %copy-start = (f32[1536,256]{1,0:T(8,128)S(1)}, f32[1536,256]{1,0:T(8,128)}, u32[]{:S(2)}) copy-start(f32[1536,256]{1,0:T(8,128)} %get-tuple-element.5) | copy-start | bytes 4718596

commit v3 on v2

v3 whole, which is shorter than its diff:
```python
import functools

import jax
import jax.numpy as jnp
import numpy as np
from jax import lax
from jax.experimental import pallas as pl
from jax.experimental.pallas import tpu as pltpu
from jax.sharding import PartitionSpec as P

SIDE = 256
ROWS = 384
MODES = 3
SCANS = 2
NX, NZ, NY = 4, 8, 4
N_TILE = 64
F32 = jnp.float32
BF16 = jnp.bfloat16
BLK = 32


def dft_blocks():
    counter = np.arange(SIDE)
    phase = (np.outer(counter, counter) % SIDE) * (2.0 * np.pi / SIDE)
    real = np.cos(phase) / np.sqrt(SIDE)
    imag = -np.sin(phase) / np.sqrt(SIDE)
    left = np.block([[real, -imag], [imag, real]])
    right = np.block([[real, imag], [-imag, real]])
    return left.astype(np.float32).astype(jnp.bfloat16), right.astype(np.float32).astype(jnp.bfloat16)


class Sems:
    def __init__(self, send, recv):
        self.send, self.recv, self.used, self.started = send, recv, 0, []

    def make(self, src, dst, dev):
        i = self.used
        self.used += 1
        copy = pltpu.make_async_remote_copy(
            src_ref=src,
            dst_ref=dst,
            send_sem=self.send.at[i],
            recv_sem=self.recv.at[i],
            device_id=dev,
            device_id_type=pl.DeviceIdType.MESH,
        )
        return copy

    def start(self, src, dst, dev):
        copy = self.make(src, dst, dev)
        copy.start()
        self.started.append(copy)
        return copy


N_SEMS = 128
Z_ORDER = (4, 3, 5, 2, 6, 1, 7, 0)


def rows(start, size):
    return pl.ds(pl.multiple_of(start, 8), size)


def shifted(blocks, rest):
    turned = pltpu.roll(blocks, (16 - rest) % 8, axis=1)
    row = lax.broadcasted_iota(jnp.int32, turned[1:].shape, 1)
    return jnp.where(row < 8 - rest, turned[:-1], turned[1:])


def kernel(
    row_ref, col_ref, cnt_ref, obj_hbm, probe_hbm, amp_hbm, lf_hbm, rf_hbm,
    onew_ref, pnew_ref,
    obj, probe_ref, amp_ref, lf_ref, rf_ref,
    border, win, psi, half, spec, power, pw, factor, pad, pgrad, p_core,
    px, pz, own, edge, from_core, ro, re, arrive,
    send_sem, recv_sem, fetch_sem,
):
    t = lax.axis_index("tile")
    y = lax.axis_index("mode")
    core = t % 2
    z = (t // 2) % NZ
    x = t // (2 * NZ)
    sems = Sems(send_sem, recv_sem)

    def tile_dev(xx, zz, cc):
        return ((xx * NZ + zz) * 2 + cc, y)

    t_left = ((t + N_TILE - 1) % N_TILE, y)
    t_right = ((t + 1) % N_TILE, y)
    peer = tile_dev(x, z, 1 - core)

    y_on = [(t, (y + k) % NY) for k in range(1, NY)]
    x_on = [tile_dev((x + k) % NX, z, core) for k in range(1, NX)]
    z_dev = [tile_dev(x, (z + k) % NZ, core) for k in range(1, NZ)]

    fetch = []
    for src, dst in ((obj_hbm, obj), (probe_hbm, probe_ref), (lf_hbm, lf_ref), (rf_hbm, rf_ref), (amp_hbm, amp_ref)):
        fetch.append(pltpu.make_async_copy(src, dst, fetch_sem.at[len(fetch)]))
        fetch[-1].start()

    barrier = pltpu.get_barrier_semaphore()
    partners = [t_left, t_right, *y_on, *x_on, *z_dev]
    for dev in partners:
        pl.semaphore_signal(barrier, inc=1, device_id=dev, device_id_type=pl.DeviceIdType.MESH)
    pl.semaphore_wait(barrier, len(partners))

    def blocks(index, first, last):
        return pl.ds(index * (ROWS // 32) + first, last - first)

    def near(ref, at):
        return ref.at[:, at]

    y_up, y_across, y_down = [(y + k) % NY for k in range(1, NY)]
    whole = sems.make(obj_hbm, border, peer)
    ranges = (blocks(y, 0, 8), blocks(y_across, 0, 12), blocks(y, 8, 12), blocks(y_up, 8, 12), blocks(y_down, 8, 12))
    direct = [sems.make(near(obj_hbm, at), near(border, at), t_left) for at in ranges]
    passed = [sems.make(near(border, ranges[0]), near(border, ranges[0]), dev) for dev in (y_on[0], y_on[2])]

    @pl.when(core == 1)
    def _():
        whole.start()

    @pl.when(core == 0)
    def _():
        for copy in direct:
            copy.start()

    for s in range(SCANS):
        for c in range(2):
            pad[s, c, 0:16] = jnp.zeros((16, 8, SIDE), F32)
            pad[s, c, 48:64] = jnp.zeros((16, 8, SIDE), F32)

    for copy in fetch:
        copy.wait()

    @pl.when(core == 1)
    def _():
        direct[0].wait_recv()
        passed[0].start()
        passed[1].start()
        for copy in (*direct[1:], *passed):
            copy.wait_recv()

    @pl.when(core == 0)
    def _():
        whole.wait_recv()

    lane = lax.broadcasted_iota(jnp.int32, (BLK // 8 + 1, 8, SIDE), 2)
    beyond = jnp.where(t == N_TILE - 1, 0.0, 1.0).astype(F32)

    def forward(s):
        top, col = row_ref[s], col_ref[s]
        base = jnp.minimum(top // 8, 15)
        rest = top - base * 8

        def cut(i, carry):
            at = pl.ds(base + i * (BLK // 8), BLK // 8 + 1)
            for c in range(2):
                block = jnp.where(lane >= col, obj[c, at], border[c, at] * beyond)
                block = pltpu.roll(shifted(block, rest), (SIDE - col) % SIDE, axis=2)
                win[s, c, rows(i * BLK, BLK), :] = block.reshape(BLK, SIDE)
            return carry

        lax.fori_loop(0, SIDE // BLK, cut, 0)

        def mode(m):
            pr, pi = probe_ref[m, :SIDE], probe_ref[m, SIDE:]
            wr, wi = win[s, 0], win[s, 1]
            psi[m, 0:SIDE, :] = (pr * wr - pi * wi).astype(BF16)
            psi[m, SIDE:, :] = (pr * wi + pi * wr).astype(BF16)
            mid = jnp.dot(lf_ref[...], psi[m], preferred_element_type=F32).astype(BF16)
            half[m, :, 0:SIDE] = mid[0:SIDE]
            half[m, :, SIDE:] = mid[SIDE:]
            out = jnp.dot(half[m], rf_ref[...], preferred_element_type=F32).astype(BF16)
            spec[s, m] = out
            wide = out.astype(F32)
            wide = wide * wide
            wide = wide[:, :SIDE] + wide[:, SIDE:]
            power[s] = wide if m == 0 else power[s] + wide

        for m in range(MODES):
            mode(m)

    n_q = SIDE // NY

    def q_rows(index):
        return rows(index * n_q, n_q)

    sums = []
    for s in range(SCANS):
        forward(s)
        sums.append([])
        for k in (2, 1, 3):
            src = power.at[s, q_rows((y + k) % NY), :]
            sums[s].append(sems.start(src, pw.at[s, k - 1], y_on[k - 1]))
    gathers = []
    for s in range(SCANS):
        for copy in sums[s]:
            copy.wait_recv()
        q = q_rows(y)
        total = power[s, q, :] + pw[s, 0] + pw[s, 1] + pw[s, 2]
        factor[s, q, :] = amp_ref[s, q, :] / jnp.maximum(jnp.sqrt(total), 0.5) - 1.0
        gathers.append([sems.start(factor.at[s, q, :], factor.at[s, q, :], y_on[k - 1]) for k in (2, 1, 3)])

    def backward(s):
        active = jnp.where(s < cnt_ref[0], 1.0, 0.0).astype(F32)

        def mode(m):
            f = factor[s]
            psi[m, 0:SIDE, :] = (spec[s, m, :, :SIDE].astype(F32) * f).astype(BF16)
            psi[m, SIDE:, :] = (spec[s, m, :, SIDE:].astype(F32) * f).astype(BF16)
            mid = jnp.dot(rf_ref[...], psi[m], preferred_element_type=F32).astype(BF16)
            half[m, :, 0:SIDE] = mid[0:SIDE]
            half[m, :, SIDE:] = mid[SIDE:]
            chi = jnp.dot(half[m], lf_ref[...], preferred_element_type=F32) * active
            cr, ci = chi[:, :SIDE], chi[:, SIDE:]
            pr, pi = probe_ref[m, :SIDE], probe_ref[m, SIDE:]
            wr, wi = win[s, 0], win[s, 1]
            gr = (pr * cr + pi * ci).reshape(SIDE // 8, 8, SIDE)
            gi = (pr * ci - pi * cr).reshape(SIDE // 8, 8, SIDE)
            pad[s, 0, 16:48] = gr if m == 0 else pad[s, 0, 16:48] + gr
            pad[s, 1, 16:48] = gi if m == 0 else pad[s, 1, 16:48] + gi
            pgr = wr * cr + wi * ci
            pgi = wr * ci - wi * cr
            if s == 0:
                pgrad[m, :SIDE] = pgr
                pgrad[m, SIDE:] = pgi
            else:
                pgrad[m, :SIDE] = pgrad[m, :SIDE] + pgr
                pgrad[m, SIDE:] = pgrad[m, SIDE:] + pgi

        return mode

    def part(index):
        return rows(index * SIDE, SIDE)

    core_sum = []
    for s in range(SCANS):
        for copy in gathers[s]:
            copy.wait_recv()
        mode = backward(s)
        for m in range(MODES):
            mode(m)
            if s == SCANS - 1:
                core_sum.append(sems.start(pgrad.at[m, part(1 - core), :], p_core.at[m], peer))

    def place(i, carry):
        for c in range(2):
            inside = outside = 0.0
            for s in range(SCANS):
                col, down = col_ref[s], 128 - row_ref[s]
                base = jnp.minimum(down // 8, 15)
                block = pad[s, c, pl.ds(base + i * (BLK // 8), BLK // 8 + 1)]
                block = pltpu.roll(shifted(block, down - base * 8), col, axis=2)
                here = lane[1:] >= col
                inside = inside + jnp.where(here, block, 0.0)
                outside = outside + jnp.where(here, 0.0, block)
            own[c, rows(i * BLK, BLK), :] = inside.reshape(BLK, SIDE)
            edge[c, rows(i * BLK, BLK), :] = outside.reshape(BLK, SIDE)
        return carry

    lax.fori_loop(0, ROWS // BLK, place, 0)

    quarter_rows = ROWS // NY

    def quarter(index):
        return rows(index * quarter_rows, quarter_rows)

    def object_flow():
        core_edge = sems.make(edge, from_core, peer)
        far = (2, 1, 3)
        edge_sum = [sems.make(edge.at[:, quarter((y + k) % NY), :], re.at[k - 1], y_on[k - 1]) for k in far]
        cross = sems.make(edge.at[:, quarter(y), :], arrive, t_right)

        @pl.when(core == 0)
        def _():
            core_edge.start()

        @pl.when(core == 1)
        def _():
            for copy in edge_sum:
                copy.start()

        yield 3.5

        @pl.when(core == 0)
        def _():
            core_edge.wait_send()

        @pl.when(core == 1)
        def _():
            core_edge.wait_recv()
            own[...] = own[...] + from_core[...]

        own_sum = []
        for c in range(2):
            for k in far:
                src = own.at[c, quarter((y + k) % NY), :]
                own_sum.append(sems.start(src, ro.at[k - 1, c], y_on[k - 1]))
        yield 8.0

        @pl.when(core == 1)
        def _():
            for copy in edge_sum:
                copy.wait_recv()
            edge[:, quarter(y), :] = edge[:, quarter(y), :] + re[0] + re[1] + re[2]
            cross.start()

        yield 14.8

        @pl.when(core == 0)
        def _():
            cross.wait_recv()

        @pl.when((core == 1) | (t == 0))
        def _():
            arrive[...] = jnp.zeros(arrive.shape, F32)

        q8 = pl.ds(y * (quarter_rows // 8), quarter_rows // 8)
        spread = []
        for c in range(2):
            for copy in own_sum[3 * c : 3 * c + 3]:
                copy.wait_recv()
            total = own[c, quarter(y), :] + ro[0, c] + ro[1, c] + ro[2, c] + arrive[c]
            onew_ref[c, quarter(y), :] = obj[c, q8].reshape(quarter_rows, SIDE) + total
            here = onew_ref.at[c, quarter(y), :]
            spread += [sems.start(here, here, y_on[k - 1]) for k in far]
        yield 27.0
        for copy in spread:
            copy.wait_recv()

        @pl.when(core == 1)
        def _():
            for copy in (*edge_sum, cross):
                copy.wait_send()

    def piece(xx, zz):
        return rows(core * SIDE + (xx * NZ + zz) * 8, 8)

    def group(xx):
        return rows(core * SIDE + xx * NZ * 8, NZ * 8)

    def same(xx, zz):
        return pnew_ref.at[:, piece(xx, zz), :]

    def probe_flow():
        yield 1.5
        for m in range(MODES):
            core_sum[m].wait_recv()
            pgrad[m, part(core), :] = pgrad[m, part(core), :] + p_core[m]
        x_sum = {}
        for k in Z_ORDER:
            for d in (2, 1, 3):
                src = pgrad.at[:, piece((x + d) % NX, (z + k) % NZ), :]
                x_sum[k, d] = sems.start(src, px.at[k, d - 1], x_on[d - 1])
        z_sum = {}
        for j, k in enumerate(Z_ORDER):
            yield 5.8 + 0.92 * j
            for d in (2, 1, 3):
                x_sum[k, d].wait_recv()
            at = piece(x, (z + k) % NZ)
            pgrad[:, at, :] = pgrad[:, at, :] + px[k, 0] + px[k, 1] + px[k, 2]
            if k:
                z_sum[k] = sems.start(pgrad.at[:, at, :], pz.at[k - 1], z_dev[k - 1])
        yield 14.5
        here = piece(x, z)
        total = pgrad[:, here, :]
        for k in Z_ORDER[:-1]:
            z_sum[k].wait_recv()
            total = total + pz[k - 1]
        pnew_ref[:, here, :] = probe_ref[:, here, :] + total * 0.5
        z_all = {k: sems.start(same(x, z), same(x, z), z_dev[k - 1]) for k in Z_ORDER[:-1]}
        x_all = {}
        for j, k in enumerate(Z_ORDER[::-1]):
            zz = (z + NZ - k) % NZ
            if k:
                yield 17.0 + 0.5 * j
                z_all[k].wait_recv()
            for d in (2, 1, 3):
                x_all[k, d] = sems.start(same(x, zz), same(x, zz), x_on[d - 1])
        core_all = [sems.start(pnew_ref.at[:, group(x), :], pnew_ref.at[:, group(x), :], peer)]
        yield 26.0
        for d in (1, 3, 2):
            for k in Z_ORDER:
                x_all[k, d].wait_recv()
            at = group((x + NX - d) % NX)
            core_all.append(sems.start(pnew_ref.at[:, at, :], pnew_ref.at[:, at, :], peer))
        yield 28.0
        for copy in core_all:
            copy.wait_recv()

    flows = [object_flow(), probe_flow()]
    due = [next(flow) for flow in flows]
    while flows:
        i = due.index(min(due))
        at = next(flows[i], None)
        if at is None:
            del flows[i], due[i]
        else:
            due[i] = at

    for copy in sems.started:
        copy.wait_send()

    @pl.when(core == 1)
    def _():
        for copy in (whole, *passed):
            copy.wait_send()

    @pl.when(core == 0)
    def _():
        for copy in direct:
            copy.wait_send()


def on_device(object_tile, probe, amplitudes, row_offsets, col_offsets, scan_count):
    left, right = dft_blocks()
    vmem = pl.BlockSpec(memory_space=pltpu.VMEM)
    smem = pl.BlockSpec(memory_space=pltpu.SMEM)
    stacked = (MODES, 2 * SIDE, SIDE)
    anywhere = pl.BlockSpec(memory_space=pl.ANY)
    scratch = [
        pltpu.VMEM((2, ROWS // 8, 8, SIDE), F32),
        pltpu.VMEM(stacked, F32),
        pltpu.VMEM((SCANS, SIDE, SIDE), F32),
        pltpu.VMEM((2 * SIDE, 2 * SIDE), BF16),
        pltpu.VMEM((2 * SIDE, 2 * SIDE), BF16),
        pltpu.VMEM((2, ROWS // 8, 8, SIDE), F32),
        pltpu.VMEM((SCANS, 2, SIDE, SIDE), F32),
        pltpu.VMEM((MODES, 2 * SIDE, SIDE), BF16),
        pltpu.VMEM((MODES, SIDE, 2 * SIDE), BF16),
        pltpu.VMEM((SCANS, MODES, SIDE, 2 * SIDE), BF16),
        pltpu.VMEM((SCANS, SIDE, SIDE), F32),
        pltpu.VMEM((SCANS, NY - 1, SIDE // NY, SIDE), F32),
        pltpu.VMEM((SCANS, SIDE, SIDE), F32),
        pltpu.VMEM((SCANS, 2, 2 * SIDE // 8, 8, SIDE), F32),
        pltpu.VMEM(stacked, F32),
        pltpu.VMEM((MODES, SIDE, SIDE), F32),
        pltpu.VMEM((NZ, NX - 1, MODES, 8, SIDE), F32),
        pltpu.VMEM((NZ - 1, MODES, 8, SIDE), F32),
        pltpu.VMEM((2, ROWS, SIDE), F32),
        pltpu.VMEM((2, ROWS, SIDE), F32),
        pltpu.VMEM((2, ROWS, SIDE), F32),
        pltpu.VMEM((NY - 1, 2, ROWS // NY, SIDE), F32),
        pltpu.VMEM((NY - 1, 2, ROWS // NY, SIDE), F32),
        pltpu.VMEM((2, ROWS // 4, SIDE), F32),
        pltpu.SemaphoreType.DMA((N_SEMS,)),
        pltpu.SemaphoreType.DMA((N_SEMS,)),
        pltpu.SemaphoreType.DMA((5,)),
    ]
    object_new, probe_new = pl.pallas_call(
        kernel,
        out_shape=(
            pltpu.VMEM(object_tile.shape, F32),
            pltpu.VMEM(stacked, F32),
        ),
        in_specs=[smem] * 3 + [anywhere] * 5,
        out_specs=(vmem, vmem),
        scratch_shapes=scratch,
        compiler_params=pltpu.CompilerParams(
            collective_id=0, has_side_effects=True, vmem_limit_bytes=56 * 1024 * 1024
        ),
        cost_estimate=pl.CostEstimate(flops=3_300_000_000, bytes_accessed=6_000_000, transcendentals=131072),
    )(
        row_offsets,
        col_offsets,
        scan_count,
        object_tile.reshape(2, ROWS // 8, 8, SIDE),
        probe.reshape(stacked),
        amplitudes,
        jnp.asarray(left),
        jnp.asarray(right),
    )
    return object_new, probe_new.reshape(probe.shape)


def solution(mesh):
    in_specs = (
        P(None, None, "tile"),
        P("mode", None, None, None),
        P("tile", None, None),
        P("tile"),
        P("tile"),
        P("tile"),
    )
    out_specs = (P(None, None, "tile"), P("mode", None, None, None))
    return jax.shard_map(on_device, mesh=mesh, in_specs=in_specs, out_specs=out_specs, check_vma=False)
```

time: 89.1 us -> 73.7 us (0.83)
  Pallas kernels: 84.3 us -> 70.3 us
  local copies, waits for them, and re-layouts: 3.33 us -> 2.02 us
    pallas_call x1, Pallas kernels: 84.3 us -> 70.3 us  [on_device(): pl.pallas_call(kernel, out_shape=(pltpu.VMEM(object_tile.shape, F32), plt...]
    unnamed x4 -> x2, local copies, waits for them, and re-layouts: 3.33 us -> 2.02 us
where the time goes in v3:
time: 73.7 us; the launch traced here: 73.6 us
  Pallas kernels  70.3 us (95%)
  local copies, waits for them, and re-layouts  2.02 us (3%)
  between operations  1.29 us (2%)
    pallas_call x1, Pallas kernels, on_device(): pl.pallas_call(kernel, out_shape=(pltpu.VMEM(object_tile.shape, F32), plt...  70.3 us
    unnamed x2, local copies, waits for them, and re-layouts  2.02 us

profile of v3, /device:TPU:1, one launch (start us, length us, event | category | flops | bytes accessed | tf_op | source)
XLA Modules:
  0.0 73.6 jit_solution(5356853170696327604)
XLA Ops:
  1.3 70.3 %shard_map.95 = (f32[2,384,256]{2,1,0:T(8,128)S(1)}, f32[3,512,256]{2,1,0:T(8,128)S(1)}) custom-call(s32[2]{0:T(128)} %row_ref.1, s32[2]{0:T(128)} %col_ref.1, s32[1]{0:T(128)S(6)} %copy.14.cnt_ref, f32[2,48,8,256]{3,2,1,0:T(8,128)} %bitcast.5, f32[3,512,256]{2,1,0:T(8,128)} %bitcast.4, f32[2,256,256]{2,1,0:T(8,128)} %amp_hbm.1, ...), custom_call_target="tpu_custom_call" | custom-call | flops 3300000000 | bytes 6000000 | tf_op jit(solution)/shard_map/pallas_call | solution.py:451
  71.6 0.9 %copy.12 = f32[2,384,256]{2,1,0:T(8,128)} copy(f32[2,384,256]{2,1,0:T(8,128)S(1)} %get-tuple-element.6) | data formatting | bytes 1572864
  72.5 1.1 %copy.13 = f32[3,2,256,256]{3,2,1,0:T(8,128)} copy(f32[3,2,256,256]{3,2,1,0:T(8,128)S(1)} %bitcast.3) | data formatting | bytes 3145728

commit v4 on v3

--- a/solution.py
+++ b/solution.py
@@ -53,7 +53,7 @@
         return copy
 
 
-N_SEMS = 128
+N_SEMS = 288
 Z_ORDER = (4, 3, 5, 2, 6, 1, 7, 0)
 
 
@@ -73,7 +73,7 @@
     obj, probe_ref, amp_ref, lf_ref, rf_ref,
     border, win, psi, half, spec, power, pw, factor, pad, pgrad, p_core,
     px, pz, own, edge, from_core, ro, re, arrive,
-    send_sem, recv_sem, fetch_sem,
+    send_sem, recv_sem, fetch_sem, known,
 ):
     t = lax.axis_index("tile")
     y = lax.axis_index("mode")
@@ -98,11 +98,16 @@
         fetch.append(pltpu.make_async_copy(src, dst, fetch_sem.at[len(fetch)]))
         fetch[-1].start()
 
+    def tell(semaphore, devices):
+        for dev in devices:
+            pl.semaphore_signal(semaphore, inc=1, device_id=dev, device_id_type=pl.DeviceIdType.MESH)
+
     barrier = pltpu.get_barrier_semaphore()
-    partners = [t_left, t_right, *y_on, *x_on, *z_dev]
-    for dev in partners:
-        pl.semaphore_signal(barrier, inc=1, device_id=dev, device_id_type=pl.DeviceIdType.MESH)
-    pl.semaphore_wait(barrier, len(partners))
+    z_next = [z_dev[0], z_dev[-1]]
+    near_by = [y_on[0], y_on[2], x_on[0], x_on[2], *z_next]
+    tell(barrier, [t_left, t_right, *near_by])
+    pl.semaphore_wait(barrier, 2 + len(near_by))
+    tell(known.at[0], near_by)
 
     def blocks(index, first, last):
         return pl.ds(index * (ROWS // 32) + first, last - first)
@@ -145,6 +150,9 @@
     def _():
         whole.wait_recv()
 
+    pl.semaphore_wait(known.at[0], len(near_by))
+    tell(known.at[1], z_next)
+
     lane = lax.broadcasted_iota(jnp.int32, (BLK // 8 + 1, 8, SIDE), 2)
     beyond = jnp.where(t == N_TILE - 1, 0.0, 1.0).astype(F32)
 
@@ -161,10 +169,10 @@
                 win[s, c, rows(i * BLK, BLK), :] = block.reshape(BLK, SIDE)
             return carry
 
-        lax.fori_loop(0, SIDE // BLK, cut, 0)
+        lax.fori_loop(0, SIDE // BLK, cut, 0, unroll=4)
 
         def mode(m):
-            pr, pi = probe_ref[m, :SIDE], probe_ref[m, SIDE:]
+            pr, pi = probe_ref[m, 0].reshape(SIDE, SIDE), probe_ref[m, 1].reshape(SIDE, SIDE)
             wr, wi = win[s, 0], win[s, 1]
             psi[m, 0:SIDE, :] = (pr * wr - pi * wi).astype(BF16)
             psi[m, SIDE:, :] = (pr * wi + pi * wr).astype(BF16)
@@ -193,6 +201,8 @@
         for k in (2, 1, 3):
             src = power.at[s, q_rows((y + k) % NY), :]
             sums[s].append(sems.start(src, pw.at[s, k - 1], y_on[k - 1]))
+    pl.semaphore_wait(known.at[1], 2)
+    tell(known.at[2], z_next)
     gathers = []
     for s in range(SCANS):
         for copy in sums[s]:
@@ -214,52 +224,54 @@
             half[m, :, SIDE:] = mid[SIDE:]
             chi = jnp.dot(half[m], lf_ref[...], preferred_element_type=F32) * active
             cr, ci = chi[:, :SIDE], chi[:, SIDE:]
-            pr, pi = probe_ref[m, :SIDE], probe_ref[m, SIDE:]
+            pr, pi = probe_ref[m, 0].reshape(SIDE, SIDE), probe_ref[m, 1].reshape(SIDE, SIDE)
             wr, wi = win[s, 0], win[s, 1]
             gr = (pr * cr + pi * ci).reshape(SIDE // 8, 8, SIDE)
             gi = (pr * ci - pi * cr).reshape(SIDE // 8, 8, SIDE)
             pad[s, 0, 16:48] = gr if m == 0 else pad[s, 0, 16:48] + gr
             pad[s, 1, 16:48] = gi if m == 0 else pad[s, 1, 16:48] + gi
-            pgr = wr * cr + wi * ci
-            pgi = wr * ci - wi * cr
+            pgr = (wr * cr + wi * ci).reshape(NZ, NX, 8, SIDE)
+            pgi = (wr * ci - wi * cr).reshape(NZ, NX, 8, SIDE)
             if s == 0:
-                pgrad[m, :SIDE] = pgr
-                pgrad[m, SIDE:] = pgi
+                pgrad[m, 0] = pgr
+                pgrad[m, 1] = pgi
             else:
-                pgrad[m, :SIDE] = pgrad[m, :SIDE] + pgr
-                pgrad[m, SIDE:] = pgrad[m, SIDE:] + pgi
+                pgrad[m, 0] = pgrad[m, 0] + pgr
+                pgrad[m, 1] = pgrad[m, 1] + pgi
 
         return mode
 
-    def part(index):
-        return rows(index * SIDE, SIDE)
+    def place(s):
+        col, down = col_ref[s], 128 - row_ref[s]
+        base = jnp.minimum(down // 8, 15)
+
+        def rows_of(i, carry):
+            at = rows(i * BLK, BLK)
+            for c in range(2):
+                block = pad[s, c, pl.ds(base + i * (BLK // 8), BLK // 8 + 1)]
+                block = pltpu.roll(shifted(block, down - base * 8), col, axis=2)
+                here = lane[1:] >= col
+                inside = jnp.where(here, block, 0.0).reshape(BLK, SIDE)
+                outside = jnp.where(here, 0.0, block).reshape(BLK, SIDE)
+                own[c, at, :] = inside if s == 0 else own[c, at, :] + inside
+                edge[c, at, :] = outside if s == 0 else edge[c, at, :] + outside
+            return carry
+
+        lax.fori_loop(0, ROWS // BLK, rows_of, 0, unroll=4)
 
     core_sum = []
     for s in range(SCANS):
         for copy in gathers[s]:
             copy.wait_recv()
+        if s == SCANS - 1:
+            pl.semaphore_wait(known.at[2], 2)
         mode = backward(s)
         for m in range(MODES):
             mode(m)
             if s == SCANS - 1:
-                core_sum.append(sems.start(pgrad.at[m, part(1 - core), :], p_core.at[m], peer))
-
-    def place(i, carry):
-        for c in range(2):
-            inside = outside = 0.0
-            for s in range(SCANS):
-                col, down = col_ref[s], 128 - row_ref[s]
-                base = jnp.minimum(down // 8, 15)
-                block = pad[s, c, pl.ds(base + i * (BLK // 8), BLK // 8 + 1)]
-                block = pltpu.roll(shifted(block, down - base * 8), col, axis=2)
-                here = lane[1:] >= col
-                inside = inside + jnp.where(here, block, 0.0)
-                outside = outside + jnp.where(here, 0.0, block)
-            own[c, rows(i * BLK, BLK), :] = inside.reshape(BLK, SIDE)
-            edge[c, rows(i * BLK, BLK), :] = outside.reshape(BLK, SIDE)
-        return carry
-
-    lax.fori_loop(0, ROWS // BLK, place, 0)
+                core_sum.append(sems.start(pgrad.at[m, 1 - core], p_core.at[m], peer))
+        if s < SCANS - 1:
+            place(s)
 
     quarter_rows = ROWS // NY
 
@@ -267,10 +279,46 @@
         return rows(index * quarter_rows, quarter_rows)
 
     def object_flow():
+        yield 0.5
+        place(SCANS - 1)
+
         core_edge = sems.make(edge, from_core, peer)
         far = (2, 1, 3)
         edge_sum = [sems.make(edge.at[:, quarter((y + k) % NY), :], re.at[k - 1], y_on[k - 1]) for k in far]
-        cross = sems.make(edge.at[:, quarter(y), :], arrive, t_right)
+        n_cross = 4
+        n_part = quarter_rows // n_cross
+        cross = []
+        for c in range(2):
+            for i in range(n_cross):
+                src = edge.at[c, rows(y * quarter_rows + i * n_part, n_part), :]
+                cross.append(sems.make(src, arrive.at[c, rows(i * n_part, n_part), :], t_right))
+        own_sum = {}
+        for c in range(2):
+            for k in far:
+                src = own.at[c, quarter((y + k) % NY), :]
+                own_sum[c, k] = sems.make(src, ro.at[k - 1, c], y_on[k - 1])
+        spread = {}
+        for c in range(2):
+            here = onew_ref.at[c, quarter(y), :]
+            for k in far:
+                spread[c, k] = sems.make(here, here, y_on[k - 1])
+        q8 = pl.ds(y * (quarter_rows // 8), quarter_rows // 8)
+        inner = jnp.where(t == 0, 0.0, 1.0).astype(F32)
+
+        def finish(c, on_core):
+            @pl.when(core == on_core)
+            def _():
+                if on_core == 0:
+                    for copy in cross[c * n_cross : (c + 1) * n_cross]:
+                        copy.wait_recv()
+                for k in far:
+                    own_sum[c, k].wait_recv()
+                total = own[c, quarter(y), :] + ro[0, c] + ro[1, c] + ro[2, c]
+                if on_core == 0:
+                    total = total + arrive[c] * inner
+                onew_ref[c, quarter(y), :] = obj[c, q8].reshape(quarter_rows, SIDE) + total
+                for k in far:
+                    spread[c, k].start()
 
         @pl.when(core == 0)
         def _():
@@ -281,7 +329,7 @@
             for copy in edge_sum:
                 copy.start()
 
-        yield 3.5
+        yield 4.5
 
         @pl.when(core == 0)
         def _():
@@ -292,104 +340,90 @@
             core_edge.wait_recv()
             own[...] = own[...] + from_core[...]
 
-        own_sum = []
-        for c in range(2):
-            for k in far:
-                src = own.at[c, quarter((y + k) % NY), :]
-                own_sum.append(sems.start(src, ro.at[k - 1, c], y_on[k - 1]))
-        yield 8.0
+        for copy in own_sum.values():
+            copy.start()
+        yield 10.0
 
         @pl.when(core == 1)
         def _():
             for copy in edge_sum:
                 copy.wait_recv()
             edge[:, quarter(y), :] = edge[:, quarter(y), :] + re[0] + re[1] + re[2]
-            cross.start()
-
-        yield 14.8
-
-        @pl.when(core == 0)
-        def _():
-            cross.wait_recv()
-
-        @pl.when((core == 1) | (t == 0))
-        def _():
-            arrive[...] = jnp.zeros(arrive.shape, F32)
-
-        q8 = pl.ds(y * (quarter_rows // 8), quarter_rows // 8)
-        spread = []
-        for c in range(2):
-            for copy in own_sum[3 * c : 3 * c + 3]:
-                copy.wait_recv()
-            total = own[c, quarter(y), :] + ro[0, c] + ro[1, c] + ro[2, c] + arrive[c]
-            onew_ref[c, quarter(y), :] = obj[c, q8].reshape(quarter_rows, SIDE) + total
-            here = onew_ref.at[c, quarter(y), :]
-            spread += [sems.start(here, here, y_on[k - 1]) for k in far]
+            cross[0].start()
+
+        for i in range(1, 2 * n_cross):
+            yield 10.0 + 0.7 * i
+            if i == 4:
+                finish(0, 1)
+
+            @pl.when(core == 1)
+            def _(copy=cross[i]):
+                copy.start()
+
+        yield 15.6
+        finish(0, 0)
+        yield 16.4
+        finish(1, 1)
+        yield 18.2
+        finish(1, 0)
         yield 27.0
-        for copy in spread:
+        for copy in spread.values():
             copy.wait_recv()
+        sems.started += [*own_sum.values(), *spread.values()]
 
         @pl.when(core == 1)
         def _():
-            for copy in (*edge_sum, cross):
+            for copy in (*edge_sum, *cross):
                 copy.wait_send()
 
-    def piece(xx, zz):
-        return rows(core * SIDE + (xx * NZ + zz) * 8, 8)
-
-    def group(xx):
-        return rows(core * SIDE + xx * NZ * 8, NZ * 8)
-
-    def same(xx, zz):
-        return pnew_ref.at[:, piece(xx, zz), :]
-
-    def probe_flow():
-        yield 1.5
-        for m in range(MODES):
-            core_sum[m].wait_recv()
-            pgrad[m, part(core), :] = pgrad[m, part(core), :] + p_core[m]
-        x_sum = {}
+    def probe_flow(m):
+        begin = 0.2 + 2.8 * m
+        grad, new = pgrad.at[m, core], pnew_ref.at[m, core]
+        yield 0.2 + 0.8 * m
+        core_sum[m].wait_recv()
+        grad[...] = grad[...] + p_core[m]
+        x_sum, z_sum = {}, {}
         for k in Z_ORDER:
             for d in (2, 1, 3):
-                src = pgrad.at[:, piece((x + d) % NX, (z + k) % NZ), :]
-                x_sum[k, d] = sems.start(src, px.at[k, d - 1], x_on[d - 1])
-        z_sum = {}
+                src = grad.at[(z + k) % NZ, (x + d) % NX]
+                x_sum[k, d] = sems.start(src, px.at[m, k, d - 1], x_on[d - 1])
         for j, k in enumerate(Z_ORDER):
-            yield 5.8 + 0.92 * j
+            yield begin + 3.7 + 0.35 * j
             for d in (2, 1, 3):
                 x_sum[k, d].wait_recv()
-            at = piece(x, (z + k) % NZ)
-            pgrad[:, at, :] = pgrad[:, at, :] + px[k, 0] + px[k, 1] + px[k, 2]
+            zz = (z + k) % NZ
+            grad[zz, x] = grad[zz, x] + px[m, k, 0] + px[m, k, 1] + px[m, k, 2]
             if k:
-                z_sum[k] = sems.start(pgrad.at[:, at, :], pz.at[k - 1], z_dev[k - 1])
-        yield 14.5
-        here = piece(x, z)
-        total = pgrad[:, here, :]
+                z_sum[k] = sems.start(grad.at[zz, x], pz.at[m, k - 1], z_dev[k - 1])
+        yield begin + 9.0
+        total = grad[z, x]
         for k in Z_ORDER[:-1]:
             z_sum[k].wait_recv()
-            total = total + pz[k - 1]
-        pnew_ref[:, here, :] = probe_ref[:, here, :] + total * 0.5
-        z_all = {k: sems.start(same(x, z), same(x, z), z_dev[k - 1]) for k in Z_ORDER[:-1]}
+            total = total + pz[m, k - 1]
+        new[z, x] = probe_ref[m, core, z, x] + total * 0.5
+
+        def share(at, dev):
+            return sems.start(new.at[at], new.at[at], dev)
+
+        core_all = []
+        z_all = {k: share((z, x), z_dev[k - 1]) for k in Z_ORDER[:-1]}
         x_all = {}
         for j, k in enumerate(Z_ORDER[::-1]):
-            zz = (z + NZ - k) % NZ
             if k:
-                yield 17.0 + 0.5 * j
+                yield begin + 11.8 + 0.3 * j
                 z_all[k].wait_recv()
             for d in (2, 1, 3):
-                x_all[k, d] = sems.start(same(x, zz), same(x, zz), x_on[d - 1])
-        core_all = [sems.start(pnew_ref.at[:, group(x), :], pnew_ref.at[:, group(x), :], peer)]
-        yield 26.0
-        for d in (1, 3, 2):
-            for k in Z_ORDER:
+                x_all[k, d] = share(((z + NZ - k) % NZ, x), x_on[d - 1])
+        for j, k in enumerate(Z_ORDER[::-1]):
+            yield begin + 15.8 + 0.3 * j
+            for d in (1, 3, 2):
                 x_all[k, d].wait_recv()
-            at = group((x + NX - d) % NX)
-            core_all.append(sems.start(pnew_ref.at[:, at, :], pnew_ref.at[:, at, :], peer))
-        yield 28.0
+            core_all.append(share(((z + NZ - k) % NZ,), peer))
+        yield begin + 19.5
         for copy in core_all:
             copy.wait_recv()
 
-    flows = [object_flow(), probe_flow()]
+    flows = [object_flow(), *(probe_flow(m) for m in range(MODES))]
     due = [next(flow) for flow in flows]
     while flows:
         i = due.index(min(due))
@@ -417,7 +451,7 @@
     left, right = dft_blocks()
     vmem = pl.BlockSpec(memory_space=pltpu.VMEM)
     smem = pl.BlockSpec(memory_space=pltpu.SMEM)
-    stacked = (MODES, 2 * SIDE, SIDE)
+    stacked = (MODES, 2, NZ, NX, 8, SIDE)
     anywhere = pl.BlockSpec(memory_space=pl.ANY)
     scratch = [
         pltpu.VMEM((2, ROWS // 8, 8, SIDE), F32),
@@ -435,9 +469,9 @@
         pltpu.VMEM((SCANS, SIDE, SIDE), F32),
         pltpu.VMEM((SCANS, 2, 2 * SIDE // 8, 8, SIDE), F32),
         pltpu.VMEM(stacked, F32),
-        pltpu.VMEM((MODES, SIDE, SIDE), F32),
-        pltpu.VMEM((NZ, NX - 1, MODES, 8, SIDE), F32),
-        pltpu.VMEM((NZ - 1, MODES, 8, SIDE), F32),
+        pltpu.VMEM((MODES, NZ, NX, 8, SIDE), F32),
+        pltpu.VMEM((MODES, NZ, NX - 1, 8, SIDE), F32),
+        pltpu.VMEM((MODES, NZ - 1, 8, SIDE), F32),
         pltpu.VMEM((2, ROWS, SIDE), F32),
         pltpu.VMEM((2, ROWS, SIDE), F32),
         pltpu.VMEM((2, ROWS, SIDE), F32),
@@ -447,6 +481,7 @@
         pltpu.SemaphoreType.DMA((N_SEMS,)),
         pltpu.SemaphoreType.DMA((N_SEMS,)),
         pltpu.SemaphoreType.DMA((5,)),
+        pltpu.SemaphoreType.REGULAR((3,)),
     ]
     object_new, probe_new = pl.pallas_call(
         kernel,

time: 73.7 us -> 68.7 us (0.932)
  Pallas kernels: 70.3 us -> 65.2 us
    pallas_call x1, Pallas kernels: 70.3 us -> 65.2 us  [on_device(): pl.pallas_call(kernel, out_shape=(pltpu.VMEM(object_tile.shape, F32), plt...]
where the time goes in v4:
time: 68.7 us; the launch traced here: 68.6 us
  Pallas kernels  65.2 us (95%)
  local copies, waits for them, and re-layouts  2.02 us (3%)
  between operations  1.29 us (2%)
    pallas_call x1, Pallas kernels, on_device(): pl.pallas_call(kernel, out_shape=(pltpu.VMEM(object_tile.shape, F32), plt...  65.2 us
    unnamed x2, local copies, waits for them, and re-layouts  2.02 us

profile of v4, /device:TPU:1, one launch (start us, length us, event | category | flops | bytes accessed | tf_op | source)
XLA Modules:
  0.0 68.6 jit_solution(9980618708297152300)
XLA Ops:
  1.3 65.2 %shard_map.95 = (f32[2,384,256]{2,1,0:T(8,128)S(1)}, f32[3,2,8,4,8,256]{5,4,3,2,1,0:T(8,128)S(1)}) custom-call(s32[2]{0:T(128)} %row_ref.1, s32[2]{0:T(128)} %col_ref.1, s32[1]{0:T(128)S(6)} %copy.14.cnt_ref, f32[2,48,8,256]{3,2,1,0:T(8,128)} %bitcast.5, f32[3,2,8,4,8,256]{5,4,3,2,1,0:T(8,128)} %bitcast.4, f32[2,256,256]{2,1,0:T(8,128)} %amp_hbm.1, ...), custom_call_target="tpu_custom_call" | custom-call | flops 3300000000 | bytes 6000000 | tf_op jit(solution)/shard_map/pallas_call | solution.py:486
  66.5 0.9 %copy.12 = f32[2,384,256]{2,1,0:T(8,128)} copy(f32[2,384,256]{2,1,0:T(8,128)S(1)} %get-tuple-element.6) | data formatting | bytes 1572864
  67.4 1.1 %copy.13 = f32[3,2,256,256]{3,2,1,0:T(8,128)} copy(f32[3,2,256,256]{3,2,1,0:T(8,128)S(1)} %bitcast.3) | data formatting | bytes 3145728

commit v5 on v4

--- a/solution.py
+++ b/solution.py
@@ -117,9 +117,10 @@
 
     y_up, y_across, y_down = [(y + k) % NY for k in range(1, NY)]
     whole = sems.make(obj_hbm, border, peer)
-    ranges = (blocks(y, 0, 8), blocks(y_across, 0, 12), blocks(y, 8, 12), blocks(y_up, 8, 12), blocks(y_down, 8, 12))
+    relayed = [blocks(y, 3 * i, 3 * i + 3) for i in range(3)]
+    ranges = (*relayed, blocks(y_across, 0, 12), *(blocks(i, 9, 12) for i in (y, y_up, y_down)))
     direct = [sems.make(near(obj_hbm, at), near(border, at), t_left) for at in ranges]
-    passed = [sems.make(near(border, ranges[0]), near(border, ranges[0]), dev) for dev in (y_on[0], y_on[2])]
+    passed = [sems.make(near(border, at), near(border, at), dev) for at in relayed for dev in (y_on[0], y_on[2])]
 
     @pl.when(core == 1)
     def _():
@@ -140,10 +141,11 @@
 
     @pl.when(core == 1)
     def _():
-        direct[0].wait_recv()
-        passed[0].start()
-        passed[1].start()
-        for copy in (*direct[1:], *passed):
+        for i in range(3):
+            direct[i].wait_recv()
+            passed[2 * i].start()
+            passed[2 * i + 1].start()
+        for copy in (*direct[3:], *passed):
             copy.wait_recv()
 
     @pl.when(core == 0)
@@ -201,8 +203,6 @@
         for k in (2, 1, 3):
             src = power.at[s, q_rows((y + k) % NY), :]
             sums[s].append(sems.start(src, pw.at[s, k - 1], y_on[k - 1]))
-    pl.semaphore_wait(known.at[1], 2)
-    tell(known.at[2], z_next)
     gathers = []
     for s in range(SCANS):
         for copy in sums[s]:
@@ -211,6 +211,8 @@
         total = power[s, q, :] + pw[s, 0] + pw[s, 1] + pw[s, 2]
         factor[s, q, :] = amp_ref[s, q, :] / jnp.maximum(jnp.sqrt(total), 0.5) - 1.0
         gathers.append([sems.start(factor.at[s, q, :], factor.at[s, q, :], y_on[k - 1]) for k in (2, 1, 3)])
+    pl.semaphore_wait(known.at[1], 2)
+    tell(known.at[2], z_next)
 
     def backward(s):
         active = jnp.where(s < cnt_ref[0], 1.0, 0.0).astype(F32)
@@ -263,8 +265,6 @@
     for s in range(SCANS):
         for copy in gathers[s]:
             copy.wait_recv()
-        if s == SCANS - 1:
-            pl.semaphore_wait(known.at[2], 2)
         mode = backward(s)
         for m in range(MODES):
             mode(m)
@@ -423,6 +423,7 @@
         for copy in core_all:
             copy.wait_recv()
 
+    pl.semaphore_wait(known.at[2], 2)
     flows = [object_flow(), *(probe_flow(m) for m in range(MODES))]
     due = [next(flow) for flow in flows]
     while flows:
@@ -506,6 +507,22 @@
         jnp.asarray(left),
         jnp.asarray(right),
     )
+
+    def leave(a, b, a_out, b_out, sem):
+        copies = [pltpu.make_async_copy(src, dst, sem.at[i]) for i, (src, dst) in enumerate(((a, a_out), (b, b_out)))]
+        for copy in copies:
+            copy.start()
+        for copy in copies:
+            copy.wait()
+
+    object_new, probe_new = pl.pallas_call(
+        leave,
+        out_shape=(jax.ShapeDtypeStruct(object_tile.shape, F32), jax.ShapeDtypeStruct(stacked, F32)),
+        in_specs=[anywhere] * 2,
+        out_specs=(anywhere, anywhere),
+        scratch_shapes=[pltpu.SemaphoreType.DMA((2,))],
+        compiler_params=pltpu.CompilerParams(vmem_limit_bytes=16 * 1024 * 1024),
+    )(object_new, probe_new)
     return object_new, probe_new.reshape(probe.shape)
 
 

time: 68.7 us -> 67.6 us (0.984)
  local copies, waits for them, and re-layouts: 2.02 us -> 0 us
  Pallas kernels: 65.2 us -> 66.2 us
    unnamed x2 -> x0, local copies, waits for them, and re-layouts: 2.02 us -> none
    pallas_call x0 -> x1, Pallas kernels: none -> 1.42 us  [on_device(): pl.pallas_call(leave, out_shape=(jax.ShapeDtypeStruct(object_tile.shape,...]
where the time goes in v5:
time: 67.6 us; the launch traced here: 67.5 us
  Pallas kernels  66.2 us (98%)
  between operations  1.29 us (2%)
    pallas_call x1, Pallas kernels, on_device(): pl.pallas_call(kernel, out_shape=(pltpu.VMEM(object_tile.shape, F32), plt...  64.8 us
    pallas_call x1, Pallas kernels, on_device(): pl.pallas_call(leave, out_shape=(jax.ShapeDtypeStruct(object_tile.shape,...  1.42 us

profile of v5, /device:TPU:1, one launch (start us, length us, event | category | flops | bytes accessed | tf_op | source)
XLA Modules:
  0.0 67.5 jit_solution(13423078522350277887)
XLA Ops:
  1.3 64.8 %shard_map.95 = (f32[2,384,256]{2,1,0:T(8,128)S(1)}, f32[3,2,8,4,8,256]{5,4,3,2,1,0:T(8,128)S(1)}) custom-call(s32[2]{0:T(128)} %row_ref.1, s32[2]{0:T(128)} %col_ref.1, s32[1]{0:T(128)S(6)} %copy.10.cnt_ref, f32[2,48,8,256]{3,2,1,0:T(8,128)} %bitcast.5, f32[3,2,8,4,8,256]{5,4,3,2,1,0:T(8,128)} %bitcast.3, f32[2,256,256]{2,1,0:T(8,128)} %amp_hbm.1, ...), custom_call_target="tpu_custom_call" | custom-call | flops 3300000000 | bytes 6000000 | tf_op jit(solution)/shard_map/pallas_call | solution.py:487
  66.1 1.4 %shard_map.96 = (f32[2,384,256]{2,1,0:T(8,128)}, f32[3,2,8,4,8,256]{5,4,3,2,1,0:T(8,128)}) custom-call(f32[2,384,256]{2,1,0:T(8,128)S(1)} %get-tuple-element.6.a, f32[3,2,8,4,8,256]{5,4,3,2,1,0:T(8,128)S(1)} %get-tuple-element.7.b), custom_call_target="tpu_custom_call" | custom-call | tf_op jit(solution)/shard_map/pallas_call | solution.py:518

commit v6 on v5

--- a/solution.py
+++ b/solution.py
@@ -31,7 +31,7 @@
 
 class Sems:
     def __init__(self, send, recv):
-        self.send, self.recv, self.used, self.started = send, recv, 0, []
+        self.send, self.recv, self.used, self.started, self.now = send, recv, 0, [], -5.0
 
     def make(self, src, dst, dev):
         i = self.used
@@ -49,8 +49,14 @@
     def start(self, src, dst, dev):
         copy = self.make(src, dst, dev)
         copy.start()
-        self.started.append(copy)
+        self.started.append((copy, self.now))
         return copy
+
+    def settle(self, now):
+        old = [copy for copy, at in self.started if at + 8.0 < now]
+        self.started = [(copy, at) for copy, at in self.started if at + 8.0 >= now]
+        for copy in old:
+            copy.wait_send()
 
 
 N_SEMS = 288
@@ -93,19 +99,18 @@
     x_on = [tile_dev((x + k) % NX, z, core) for k in range(1, NX)]
     z_dev = [tile_dev(x, (z + k) % NZ, core) for k in range(1, NZ)]
 
+    def tell(semaphore, devices):
+        for dev in devices:
+            pl.semaphore_signal(semaphore, inc=1, device_id=dev, device_id_type=pl.DeviceIdType.MESH)
+
+    barrier = pltpu.get_barrier_semaphore()
+    z_next = [z_dev[0], z_dev[-1]]
+    near_by = [y_on[0], y_on[2], x_on[0], x_on[2], *z_next]
+    tell(barrier, [t_left, t_right, *near_by])
     fetch = []
     for src, dst in ((obj_hbm, obj), (probe_hbm, probe_ref), (lf_hbm, lf_ref), (rf_hbm, rf_ref), (amp_hbm, amp_ref)):
         fetch.append(pltpu.make_async_copy(src, dst, fetch_sem.at[len(fetch)]))
         fetch[-1].start()
-
-    def tell(semaphore, devices):
-        for dev in devices:
-            pl.semaphore_signal(semaphore, inc=1, device_id=dev, device_id_type=pl.DeviceIdType.MESH)
-
-    barrier = pltpu.get_barrier_semaphore()
-    z_next = [z_dev[0], z_dev[-1]]
-    near_by = [y_on[0], y_on[2], x_on[0], x_on[2], *z_next]
-    tell(barrier, [t_left, t_right, *near_by])
     pl.semaphore_wait(barrier, 2 + len(near_by))
     tell(known.at[0], near_by)
 
@@ -171,7 +176,7 @@
                 win[s, c, rows(i * BLK, BLK), :] = block.reshape(BLK, SIDE)
             return carry
 
-        lax.fori_loop(0, SIDE // BLK, cut, 0, unroll=4)
+        lax.fori_loop(0, SIDE // BLK, cut, 0, unroll=8)
 
         def mode(m):
             pr, pi = probe_ref[m, 0].reshape(SIDE, SIDE), probe_ref[m, 1].reshape(SIDE, SIDE)
@@ -207,16 +212,16 @@
     for s in range(SCANS):
         for copy in sums[s]:
             copy.wait_recv()
+        active = jnp.where(s < cnt_ref[0], 1.0, 0.0).astype(F32)
         q = q_rows(y)
         total = power[s, q, :] + pw[s, 0] + pw[s, 1] + pw[s, 2]
         factor[s, q, :] = amp_ref[s, q, :] / jnp.maximum(jnp.sqrt(total), 0.5) - 1.0
+        factor[s, q, :] = factor[s, q, :] * active
         gathers.append([sems.start(factor.at[s, q, :], factor.at[s, q, :], y_on[k - 1]) for k in (2, 1, 3)])
     pl.semaphore_wait(known.at[1], 2)
     tell(known.at[2], z_next)
 
     def backward(s):
-        active = jnp.where(s < cnt_ref[0], 1.0, 0.0).astype(F32)
-
         def mode(m):
             f = factor[s]
             psi[m, 0:SIDE, :] = (spec[s, m, :, :SIDE].astype(F32) * f).astype(BF16)
@@ -224,7 +229,7 @@
             mid = jnp.dot(rf_ref[...], psi[m], preferred_element_type=F32).astype(BF16)
             half[m, :, 0:SIDE] = mid[0:SIDE]
             half[m, :, SIDE:] = mid[SIDE:]
-            chi = jnp.dot(half[m], lf_ref[...], preferred_element_type=F32) * active
+            chi = jnp.dot(half[m], lf_ref[...], preferred_element_type=F32)
             cr, ci = chi[:, :SIDE], chi[:, SIDE:]
             pr, pi = probe_ref[m, 0].reshape(SIDE, SIDE), probe_ref[m, 1].reshape(SIDE, SIDE)
             wr, wi = win[s, 0], win[s, 1]
@@ -333,15 +338,19 @@
 
         @pl.when(core == 0)
         def _():
-            core_edge.wait_send()
+            for copy in (*direct, core_edge):
+                copy.wait_send()
 
         @pl.when(core == 1)
         def _():
+            for copy in (whole, *passed):
+                copy.wait_send()
             core_edge.wait_recv()
             own[...] = own[...] + from_core[...]
 
         for copy in own_sum.values():
             copy.start()
+        sems.started += [(copy, sems.now + 8.0) for copy in own_sum.values()]
         yield 10.0
 
         @pl.when(core == 1)
@@ -352,8 +361,8 @@
             cross[0].start()
 
         for i in range(1, 2 * n_cross):
-            yield 10.0 + 0.7 * i
-            if i == 4:
+            yield 10.0 + 0.35 * i
+            if i == 7:
                 finish(0, 1)
 
             @pl.when(core == 1)
@@ -366,15 +375,16 @@
         finish(1, 1)
         yield 18.2
         finish(1, 0)
-        yield 27.0
-        for copy in spread.values():
-            copy.wait_recv()
-        sems.started += [*own_sum.values(), *spread.values()]
+        sems.started += [(copy, sems.now) for copy in spread.values()]
 
         @pl.when(core == 1)
         def _():
             for copy in (*edge_sum, *cross):
                 copy.wait_send()
+
+        yield 27.0
+        for copy in spread.values():
+            copy.wait_recv()
 
     def probe_flow(m):
         begin = 0.2 + 2.8 * m
@@ -425,27 +435,18 @@
 
     pl.semaphore_wait(known.at[2], 2)
     flows = [object_flow(), *(probe_flow(m) for m in range(MODES))]
+    sems.now = 0.0
     due = [next(flow) for flow in flows]
     while flows:
         i = due.index(min(due))
+        sems.now = due[i]
+        sems.settle(sems.now)
         at = next(flows[i], None)
         if at is None:
             del flows[i], due[i]
         else:
             due[i] = at
-
-    for copy in sems.started:
-        copy.wait_send()
-
-    @pl.when(core == 1)
-    def _():
-        for copy in (whole, *passed):
-            copy.wait_send()
-
-    @pl.when(core == 0)
-    def _():
-        for copy in direct:
-            copy.wait_send()
+    sems.settle(1000.0)
 
 
 def on_device(object_tile, probe, amplitudes, row_offsets, col_offsets, scan_count):

time: 67.6 us -> 66.8 us (0.988)
  Pallas kernels: 66.2 us -> 65.4 us
    pallas_call x1, Pallas kernels: 64.8 us -> 63.9 us  [on_device(): pl.pallas_call(kernel, out_shape=(pltpu.VMEM(object_tile.shape, F32), plt...]
where the time goes in v6:
time: 66.8 us; the launch traced here: 66.7 us
  Pallas kernels  65.4 us (98%)
  between operations  1.29 us (2%)
    pallas_call x1, Pallas kernels, on_device(): pl.pallas_call(kernel, out_shape=(pltpu.VMEM(object_tile.shape, F32), plt...  63.9 us
    pallas_call x1, Pallas kernels, on_device(): pl.pallas_call(leave, out_shape=(jax.ShapeDtypeStruct(object_tile.shape,...  1.42 us

profile of v6, /device:TPU:1, one launch (start us, length us, event | category | flops | bytes accessed | tf_op | source)
XLA Modules:
  0.0 66.7 jit_solution(8564865631282526208)
XLA Ops:
  1.3 63.9 %shard_map.95 = (f32[2,384,256]{2,1,0:T(8,128)S(1)}, f32[3,2,8,4,8,256]{5,4,3,2,1,0:T(8,128)S(1)}) custom-call(s32[2]{0:T(128)} %row_ref.1, s32[2]{0:T(128)} %col_ref.1, s32[1]{0:T(128)S(6)} %copy.10.cnt_ref, f32[2,48,8,256]{3,2,1,0:T(8,128)} %bitcast.5, f32[3,2,8,4,8,256]{5,4,3,2,1,0:T(8,128)} %bitcast.3, f32[2,256,256]{2,1,0:T(8,128)} %amp_hbm.1, ...), custom_call_target="tpu_custom_call" | custom-call | flops 3300000000 | bytes 6000000 | tf_op jit(solution)/shard_map/pallas_call | solution.py:488
  65.2 1.4 %shard_map.96 = (f32[2,384,256]{2,1,0:T(8,128)}, f32[3,2,8,4,8,256]{5,4,3,2,1,0:T(8,128)}) custom-call(f32[2,384,256]{2,1,0:T(8,128)S(1)} %get-tuple-element.6.a, f32[3,2,8,4,8,256]{5,4,3,2,1,0:T(8,128)S(1)} %get-tuple-element.7.b), custom_call_target="tpu_custom_call" | custom-call | tf_op jit(solution)/shard_map/pallas_call | solution.py:519

commit v7 on v6

--- a/solution.py
+++ b/solution.py
@@ -53,8 +53,8 @@
         return copy
 
     def settle(self, now):
-        old = [copy for copy, at in self.started if at + 8.0 < now]
-        self.started = [(copy, at) for copy, at in self.started if at + 8.0 >= now]
+        old = [copy for copy, at in self.started if at + 5.5 < now]
+        self.started = [(copy, at) for copy, at in self.started if at + 5.5 >= now]
         for copy in old:
             copy.wait_send()
 
@@ -264,7 +264,7 @@
                 edge[c, at, :] = outside if s == 0 else edge[c, at, :] + outside
             return carry
 
-        lax.fori_loop(0, ROWS // BLK, rows_of, 0, unroll=4)
+        lax.fori_loop(0, ROWS // BLK, rows_of, 0, unroll=12)
 
     core_sum = []
     for s in range(SCANS):

time: 66.8 us -> 67.7 us (1.013)
  Pallas kernels: 65.4 us -> 66.3 us
    pallas_call x1, Pallas kernels: 63.9 us -> 64.9 us  [on_device(): pl.pallas_call(kernel, out_shape=(pltpu.VMEM(object_tile.shape, F32), plt...]
where the time goes in v7:
time: 67.7 us; the launch traced here: 67.6 us
  Pallas kernels  66.3 us (98%)
  between operations  1.29 us (2%)
    pallas_call x1, Pallas kernels, on_device(): pl.pallas_call(kernel, out_shape=(pltpu.VMEM(object_tile.shape, F32), plt...  64.9 us
    pallas_call x1, Pallas kernels, on_device(): pl.pallas_call(leave, out_shape=(jax.ShapeDtypeStruct(object_tile.shape,...  1.42 us

profile of v7, /device:TPU:1, one launch (start us, length us, event | category | flops | bytes accessed | tf_op | source)
XLA Modules:
  0.0 67.6 jit_solution(4741494167267832544)
XLA Ops:
  1.3 64.9 %shard_map.95 = (f32[2,384,256]{2,1,0:T(8,128)S(1)}, f32[3,2,8,4,8,256]{5,4,3,2,1,0:T(8,128)S(1)}) custom-call(s32[2]{0:T(128)} %row_ref.1, s32[2]{0:T(128)} %col_ref.1, s32[1]{0:T(128)S(6)} %copy.10.cnt_ref, f32[2,48,8,256]{3,2,1,0:T(8,128)} %bitcast.5, f32[3,2,8,4,8,256]{5,4,3,2,1,0:T(8,128)} %bitcast.3, f32[2,256,256]{2,1,0:T(8,128)} %amp_hbm.1, ...), custom_call_target="tpu_custom_call" | custom-call | flops 3300000000 | bytes 6000000 | tf_op jit(solution)/shard_map/pallas_call | solution.py:488
  66.2 1.4 %shard_map.96 = (f32[2,384,256]{2,1,0:T(8,128)}, f32[3,2,8,4,8,256]{5,4,3,2,1,0:T(8,128)}) custom-call(f32[2,384,256]{2,1,0:T(8,128)S(1)} %get-tuple-element.6.a, f32[3,2,8,4,8,256]{5,4,3,2,1,0:T(8,128)S(1)} %get-tuple-element.7.b), custom_call_target="tpu_custom_call" | custom-call | tf_op jit(solution)/shard_map/pallas_call | solution.py:519
